TPU v7x, 512 devices: a whole 4x8x8 slice. The times are simulated.
512 devices in a mesh: row: 16 (over y_lo, x, core), col: 32 (over y_hi, z).
Axes of the slice: x: 4, y: 8 (y_hi: 4, y_lo: 2; y = y_hi * 2 + y_lo), z: 8, core: 2. Of those that a mesh axis runs over, the one named last changes fastest.
Arguments:
- x_in: bfloat16 [512, 12288], P('row', 'col'), may hold values from -18 to 18
- query: bfloat16 [512, 12288], P(('row', 'col')), may hold values from -6 to 6
- latest_key_value: bfloat16 [512, 2, 1024], P(('row', 'col')), may hold values from -6 to 6
- key_value_cache: bfloat16 [512, 2, 256, 1024], P(('row', 'col')), may hold values from -6 to 6
- lengths: int32 [512], P(('row', 'col')), may hold values from 2 to 256, as said below
- o_weight: bfloat16 [12288, 12288], P('row', 'col'), may hold values from -127 to 127
- o_scale: float32 [12288], P('col'), may hold values from 0.00049430673 to 0.001977227
- ffn_gain: float32 [12288], P('col'), may hold values from 0.25 to 1.75
- gate_up_weight: bfloat16 [2, 12288, 18432], P(None, 'col', 'row'), may hold values from -127 to 127
- gate_up_scale: float32 [2, 18432], P(None, 'row'), may hold values from 6.178834e-05 to 0.00024715337
- down_weight: bfloat16 [18432, 12288], P('row', 'col'), may hold values from -127 to 127
- down_scale: float32 [12288], P('col'), may hold values from 0.00010089994 to 0.00040359976
Outputs:
- x_out: bfloat16 [512, 12288], P('row', 'col')
Inputs may be any that keep to these rules, and one draw needn't show every extreme that they name: `lengths`: some row uses all 256 slots.
All inputs are finite; a program needn't handle non-finite values.
Results may differ from a plain program's by a relative error of at most 0.029.
Values may be sent and summed in bfloat16 or wider, within the bound.
No kernel may reach another device: no remote copies, remote signals or barrier semaphores. Data moves between devices by JAX's collectives and lax.ppermute only.
A program may use at most 64 MiB of HBM per device.

v0:
```python
import jax
import jax.numpy as jnp
from jax import lax
from jax.sharding import PartitionSpec as P

D = 12288
QUERY_HEADS = 96
KEY_VALUE_HEADS = 8
HEAD_SIZE = 128
CONTEXT_SLOTS = 256


def attend_local(query, latest_key_value, key_value_cache, lengths):
    slot_count = query.shape[0]
    query_group = QUERY_HEADS // KEY_VALUE_HEADS
    scale = HEAD_SIZE ** (-0.5)
    query_rows = query.reshape(slot_count, KEY_VALUE_HEADS, query_group, HEAD_SIZE)
    key_rows = key_value_cache[:, 0].reshape(slot_count, CONTEXT_SLOTS, KEY_VALUE_HEADS, HEAD_SIZE)
    value_rows = key_value_cache[:, 1].reshape(
        slot_count, CONTEXT_SLOTS, KEY_VALUE_HEADS, HEAD_SIZE
    )
    latest_keys = latest_key_value[:, 0].reshape(slot_count, KEY_VALUE_HEADS, HEAD_SIZE)
    latest_values = latest_key_value[:, 1].reshape(slot_count, KEY_VALUE_HEADS, HEAD_SIZE)
    cached = (
        jnp.einsum("akgd,apkd->akgp", query_rows, key_rows, preferred_element_type=jnp.float32)
        * scale
    )
    fresh = (
        jnp.einsum("akgd,akd->akg", query_rows, latest_keys, preferred_element_type=jnp.float32)
        * scale
    )
    position = jnp.arange(CONTEXT_SLOTS, dtype=jnp.int32)
    valid = position[None, :] < lengths[:, None]
    cached = jnp.where(valid[:, None, None, :], cached, -jnp.inf)
    top = jnp.maximum(jnp.max(cached, axis=3), fresh)
    weight_cached = jnp.exp(cached - top[..., None])
    weight_fresh = jnp.exp(fresh - top)
    total = jnp.sum(weight_cached, axis=3) + weight_fresh
    probs_cached = (weight_cached / total[..., None]).astype(jnp.bfloat16)
    probs_fresh = (weight_fresh / total).astype(jnp.bfloat16)
    mixed = jnp.einsum(
        "akgp,apkd->akgd", probs_cached, value_rows, preferred_element_type=jnp.float32
    )
    mixed = (
        mixed
        + probs_fresh.astype(jnp.float32)[..., None]
        * latest_values.astype(jnp.float32)[:, :, None, :]
    )
    return mixed.reshape(slot_count, QUERY_HEADS * HEAD_SIZE).astype(jnp.bfloat16)


def body(
    x_in,
    query,
    latest_key_value,
    key_value_cache,
    lengths,
    o_weight,
    o_scale,
    ffn_gain,
    gate_up_weight,
    gate_up_scale,
    down_weight,
    down_scale,
):
    attn_local = attend_local(query, latest_key_value, key_value_cache, lengths)
    collected = lax.all_gather(attn_local, "col", axis=0, tiled=True)
    columns = lax.all_to_all(collected, "row", split_axis=1, concat_axis=0, tiled=True)
    attended = lax.psum_scatter(
        jnp.dot(columns, o_weight, preferred_element_type=jnp.float32),
        "row",
        scatter_dimension=0,
        tiled=True,
    )
    stream = x_in.astype(jnp.float32) + attended * o_scale
    squares = lax.psum(jnp.sum(stream * stream, axis=1), "col")
    normed = (stream * lax.rsqrt(squares / D + 1e-05)[:, None] * ffn_gain).astype(jnp.bfloat16)
    partial_value = jnp.einsum(
        "rd,kdf->krf",
        lax.all_gather(normed, "row", axis=0, tiled=True),
        gate_up_weight,
        preferred_element_type=jnp.float32,
    )
    shares = lax.psum_scatter(
        partial_value.astype(jnp.bfloat16), "col", scatter_dimension=1, tiled=True
    ).astype(jnp.float32)
    gate_part = shares[0] * gate_up_scale[0]
    up_part = shares[1] * gate_up_scale[1]
    hidden = (jax.nn.silu(gate_part) * up_part).astype(jnp.bfloat16)
    products = jnp.dot(
        lax.all_gather(hidden, "col", axis=0, tiled=True),
        down_weight,
        preferred_element_type=jnp.float32,
    )
    lowered = lax.psum_scatter(products, "row", scatter_dimension=0, tiled=True)
    return (stream + lowered * down_scale).astype(jnp.bfloat16)


def solution(mesh):
    in_specs = (
        P("row", "col"),
        P(("row", "col"), None),
        P(("row", "col"), None, None),
        P(("row", "col"), None, None, None),
        P(("row", "col")),
        P("row", "col"),
        P("col"),
        P("col"),
        P(None, "col", "row"),
        P(None, "row"),
        P("row", "col"),
        P("col"),
    )
    out_specs = P("row", "col")
    return jax.shard_map(body, mesh=mesh, in_specs=in_specs, out_specs=out_specs, check_vma=False)
```

profile of v0, /device:TPU:1, one launch (start us, length us, event | category | flops | bytes accessed | tf_op | source)
XLA Modules:
  0.0 668.6 jit_solution(4390956409239347491)
XLA Ops:
  6.5 1.4 fusion.16
  7.9 0.2 copy.27
  8.2 0.1 reduce.4
  9.0 0.1 fusion.11
  9.1 0.3 fusion.17
  9.4 0.2 fusion.4
  9.6 0.2 copy.28
  9.8 0.3 fusion.2
  10.2 87.7 %all-gather = bf16[32,1,12288]{2,1,0:T(2,128)(2,1)S(1)} all-gather(bf16[1,1,12288]{2,1,0:T(2,128)(2,1)S(1)} %reshape.108), channel_id=1, replica_groups=mesh['row'=16,'col'=32] {'col'}, dimensions={0}, use_global_device_ids=true | all-gather | bytes 811008 | tf_op jit(solution)/shard_map/all_gather | solution.py:67
  97.9 5.9 reduce.5
  103.7 1.3 copy.31
  105.0 32.8 %all_to_all.19 = bf16[32,16,768]{2,0,1:T(8,128)(2,1)S(1)} all-to-all(bf16[32,16,768]{2,0,1:T(8,128)(2,1)S(1)} %bitcast.46), channel_id=1, replica_groups=mesh['row'=16,'col'=32] {'row'}, dimensions={1} | all-to-all | bytes 1572864 | tf_op jit(solution)/shard_map/all_to_all | solution.py:68
  137.8 1.5 fusion.18
  139.3 0.0 reduce-scatter.4.cloned.1.call-update
  139.3 0.0 reduce-scatter.6.cloned.1.call-start
  139.4 55.2 %reduce-scatter.4.cloned.1.call-done = f32[32,384]{1,0:T(8,128)} async-done(((f32[512,384]{1,0:T(8,128)}), f32[32,384]{1,0:T(8,128)}) %reduce-scatter.4.cloned.1.call-update) | async-done | bytes 49168 | tf_op jit(solution)/shard_map/reduce_scatter | solution.py:69
  194.6 0.9 multiply_reduce_fusion
  195.5 68.9 %psum.7 = f32[32]{0:T(128)S(1)} all-reduce(f32[32]{0:T(128)S(1)} %multiply_reduce_fusion), channel_id=1, replica_groups=mesh['row'=16,'col'=32] {'col'}, use_global_device_ids=true, to_apply=%region_4.5 | all-reduce | flops 32 | bytes 256 | tf_op jit(solution)/shard_map/psum | solution.py:76
  264.5 0.9 multiply_convert_fusion
  265.4 34.1 %all_gather.10 = bf16[512,384]{1,0:T(8,128)(2,1)S(1)} all-gather(bf16[32,384]{1,0:T(8,128)(2,1)S(1)} %multiply_convert_fusion), channel_id=1, replica_groups=mesh['row'=16,'col'=32] {'row'}, dimensions={0}, use_global_device_ids=true | all-gather | bytes 417792 | tf_op jit(solution)/shard_map/all_gather | solution.py:80
  299.5 2.8 fusion
  302.3 0.0 all-gather.3.cloned.1.call-start
  302.4 0.6 copy-done.6
  303.0 206.2 %reduce-scatter.6.cloned.1.call-done = bf16[2,16,1152]{2,1,0:T(8,128)(2,1)} async-done(((bf16[2,512,1152]{2,1,0:T(8,128)(2,1)}), bf16[2,16,1152]{2,1,0:T(8,128)(2,1)}) %reduce-scatter.6.cloned.1.call-update) | async-done | bytes 73744 | tf_op jit(solution)/shard_map/reduce_scatter | solution.py:84
  509.2 0.9 convert_element_type.70
  510.1 0.7 fusion.7
  510.8 0.0 all-gather.3.cloned.1.call-update
  510.8 0.0 reduce-scatter.8.cloned.1.call-start
  510.9 82.3 %all-gather.3.cloned.1.call-done = bf16[512,1152]{1,0:T(8,128)(2,1)} async-done(((bf16[16,1152]{1,0:T(8,128)(2,1)}), bf16[512,1152]{1,0:T(8,128)(2,1)}) %all-gather.3.cloned.1.call-update) | async-done | bytes 1179664 | tf_op jit(solution)/shard_map/all_gather | solution.py:91
  593.2 3.0 fusion.19
  596.2 64.4 %reduce-scatter.8.cloned.1.call-done = f32[32,384]{1,0:T(8,128)} async-done(((f32[512,384]{1,0:T(8,128)}), f32[32,384]{1,0:T(8,128)}) %reduce-scatter.8.cloned.1.call-update) | async-done | bytes 49168 | tf_op jit(solution)/shard_map/reduce_scatter | solution.py:95
  660.6 1.4 add_convert_fusion
  (32 shorter events, 0.2 us)
Async XLA Ops:
  6.5 293.0 %copy-start = (bf16[2,384,1152]{2,1,0:T(8,128)(2,1)S(1)}, bf16[2,384,1152]{2,1,0:T(8,128)(2,1)}, u32[]{:S(2)}) copy-start(bf16[2,384,1152]{2,1,0:T(8,128)(2,1)} %param.20) | copy-start | bytes 5308420
  6.5 1.6 copy-start.4
  6.5 2.4 copy-start.7
  6.5 188.1 %reduce-scatter.4.cloned.1.call-start = ((), (), s32[]{:S(2)}) async-start(), calls=%async_computation.4 | async-start | bytes 835584 | tf_op jit(solution)/shard_map/reduce_scatter | solution.py:69
  103.7 34.1 %copy-start.1 = (bf16[768,384]{1,0:T(8,128)(2,1)S(1)}, bf16[768,384]{1,0:T(8,128)(2,1)}, u32[]{:S(2)}) copy-start(bf16[768,384]{1,0:T(8,128)(2,1)} %param.17) | copy-start | bytes 1769476
  137.8 56.8 %copy-start.3 = (bf16[32,384]{1,0:T(8,128)(2,1)S(1)}, bf16[32,384]{1,0:T(8,128)(2,1)}, u32[]{:S(2)}) copy-start(bf16[32,384]{1,0:T(8,128)(2,1)} %param.12) | copy-start | bytes 73732
  137.8 56.8 %copy-start.5 = (f32[384]{0:T(512)S(1)}, f32[384]{0:T(512)}, u32[]{:S(2)}) copy-start(f32[384]{0:T(512)} %param.18) | copy-start | bytes 4612
  137.8 126.7 %copy-start.9 = (f32[384]{0:T(512)S(1)}, f32[384]{0:T(512)}, u32[]{:S(2)}) copy-start(f32[384]{0:T(512)} %param.19) | copy-start | bytes 4612
  139.3 369.9 %reduce-scatter.6.cloned.1.call-start = ((), (), s32[]{:S(2)}) async-start(), calls=%async_computation.5 | async-start | bytes 2433024 | tf_op jit(solution)/shard_map/reduce_scatter | solution.py:84
  302.3 0.7 copy-start.6
  302.3 290.9 %copy-start.10 = (bf16[1152,384]{1,0:T(8,128)(2,1)S(1)}, bf16[1152,384]{1,0:T(8,128)(2,1)}, u32[]{:S(2)}) copy-start(bf16[1152,384]{1,0:T(8,128)(2,1)} %param.22) | copy-start | bytes 2654212
  302.3 290.9 %all-gather.3.cloned.1.call-start = ((), (), s32[]{:S(2)}) async-start(), calls=%async_computation.6 | async-start | bytes 1216512 | tf_op jit(solution)/shard_map/all_gather | solution.py:91
  510.8 149.8 %copy-start.2 = (f32[32,384]{1,0:T(8,128)S(1)}, f32[32,384]{1,0:T(8,128)}, u32[]{:S(2)}) copy-start(f32[32,384]{1,0:T(8,128)} %reduce-scatter.4.cloned.1.call-done) | copy-start | bytes 147460
  510.8 149.8 %copy-start.8 = (f32[384]{0:T(512)S(1)}, f32[384]{0:T(512)}, u32[]{:S(2)}) copy-start(f32[384]{0:T(512)} %param.23) | copy-start | bytes 4612
  510.8 149.8 %reduce-scatter.8.cloned.1.call-start = ((), (), s32[]{:S(2)}) async-start(), calls=%async_computation.7 | async-start | bytes 835584 | tf_op jit(solution)/shard_map/reduce_scatter | solution.py:95
Sparse Core Ops, SparseCore 0:
  139.4 55.1 reduce-scatter.3
  302.4 206.7 reduce-scatter.5
  512.4 80.7 all-gather.2
  596.3 64.2 reduce-scatter.7
where the time goes:
time: 671 us; the launch traced here: 669 us
  waiting for transfers between devices  408 us (61%)
  blocking collectives  224 us (33%)
  between operations  13.9 us (2%)
  other arithmetic  11 us (2%)
  matrix products  7.97 us (1%)
    reduce_scatter x1, waiting for transfers between devices, body(): lax.psum_scatter(partial_value.astype(jnp.bfloat16), 'col', scatter_dimen...  206 us
    all_gather x1, blocking collectives, body(): collected = lax.all_gather(attn_local, 'col', axis=0, tiled=True)  87.7 us
    all_gather x1, waiting for transfers between devices, body(): lax.all_gather(hidden, 'col', axis=0, tiled=True)  82.3 us
    psum x1, blocking collectives, body(): squares = lax.psum(jnp.sum(stream * stream, axis=1), 'col')  68.9 us
    reduce_scatter x1, waiting for transfers between devices, body(): lowered = lax.psum_scatter(products, 'row', scatter_dimension=0, tiled=True)  64.4 us
    reduce_scatter x1, waiting for transfers between devices, body(): lax.psum_scatter(jnp.dot(columns, o_weight, preferred_element_type=jnp.fl...  55.2 us
    all_gather x1, blocking collectives, body(): lax.all_gather(normed, 'row', axis=0, tiled=True)  34.1 us
    all_to_all x1, blocking collectives, body(): lax.all_to_all(collected, 'row', split_axis=1, concat_axis=0, tiled=True)  32.8 us
  transfers between devices with their start and end apart: 4, of which 4 were waited for; matrix products, arithmetic and copies ran while one was open for 0% of the time, Pallas kernels for 0%

commit v1 on v0

v1 whole, which is shorter than its diff:
```python
import jax
import jax.numpy as jnp
from jax import lax
from jax.sharding import Mesh
from jax.sharding import PartitionSpec as P

D = 12288
QUERY_HEADS = 96
KEY_VALUE_HEADS = 8
HEAD_SIZE = 128
CONTEXT_SLOTS = 256
UNITS = 1152
WIDTH = 384

ROWS = ("ylo", "x", "core")
COLS = ("b", "zl")
SIDE = ("zl", "ylo", "x")
bf16 = jnp.bfloat16
f32 = jnp.float32


def attend_local(query, latest_key_value, key_value_cache, lengths):
    slot_count = query.shape[0]
    query_group = QUERY_HEADS // KEY_VALUE_HEADS
    scale = HEAD_SIZE ** (-0.5)
    query_rows = query.reshape(slot_count, KEY_VALUE_HEADS, query_group, HEAD_SIZE)
    key_rows = key_value_cache[:, 0].reshape(slot_count, CONTEXT_SLOTS, KEY_VALUE_HEADS, HEAD_SIZE)
    value_rows = key_value_cache[:, 1].reshape(
        slot_count, CONTEXT_SLOTS, KEY_VALUE_HEADS, HEAD_SIZE
    )
    latest_keys = latest_key_value[:, 0].reshape(slot_count, KEY_VALUE_HEADS, HEAD_SIZE)
    latest_values = latest_key_value[:, 1].reshape(slot_count, KEY_VALUE_HEADS, HEAD_SIZE)
    cached = (
        jnp.einsum("akgd,apkd->akgp", query_rows, key_rows, preferred_element_type=jnp.float32)
        * scale
    )
    fresh = (
        jnp.einsum("akgd,akd->akg", query_rows, latest_keys, preferred_element_type=jnp.float32)
        * scale
    )
    position = jnp.arange(CONTEXT_SLOTS, dtype=jnp.int32)
    valid = position[None, :] < lengths[:, None]
    cached = jnp.where(valid[:, None, None, :], cached, -jnp.inf)
    top = jnp.maximum(jnp.max(cached, axis=3), fresh)
    weight_cached = jnp.exp(cached - top[..., None])
    weight_fresh = jnp.exp(fresh - top)
    total = jnp.sum(weight_cached, axis=3) + weight_fresh
    probs_cached = (weight_cached / total[..., None]).astype(jnp.bfloat16)
    probs_fresh = (weight_fresh / total).astype(jnp.bfloat16)
    mixed = jnp.einsum(
        "akgp,apkd->akgd", probs_cached, value_rows, preferred_element_type=jnp.float32
    )
    mixed = (
        mixed
        + probs_fresh.astype(jnp.float32)[..., None]
        * latest_values.astype(jnp.float32)[:, :, None, :]
    )
    return mixed.reshape(slot_count, QUERY_HEADS * HEAD_SIZE).astype(jnp.bfloat16)


def swap(block):
    return lax.ppermute(block, ("core", "zl"), [(0, 0), (1, 2), (2, 1), (3, 3)])


def both(block):
    return lax.all_gather(block, "core", axis=0, tiled=False)


def exchange(parts, axis):
    return lax.all_to_all(parts, axis, split_axis=0, concat_axis=0, tiled=False)


def spread(block, axis, count):
    return exchange(jnp.broadcast_to(block[None], (count,) + block.shape), axis)


def high_low(value):
    high = value.astype(bf16)
    low = (value - high.astype(f32)).astype(bf16)
    return high, low


def body(
    x_in,
    query,
    latest_key_value,
    key_value_cache,
    lengths,
    o_weight,
    o_scale,
    ffn_gain,
    gate_up_weight,
    gate_up_scale,
    down_weight,
    down_scale,
):
    scale_high, scale_low = high_low(gate_up_scale)
    gate_up_block = jnp.concatenate(
        [
            gate_up_weight.reshape(2 * WIDTH, UNITS),
            scale_high,
            scale_low,
            jnp.zeros((12, UNITS), bf16),
        ],
        axis=0,
    )
    o_blocks = both(swap(o_weight))
    gate_up_blocks = both(swap(gate_up_block))
    down_blocks = both(swap(down_weight))

    attn = attend_local(query, latest_key_value, key_value_cache, lengths)
    attn = attn.reshape(8, 2, 768).transpose(1, 0, 2).reshape(16, 768)
    attn = exchange(attn, SIDE)
    attn = spread(attn, "b", 16)
    attn = attn.reshape(16, 2, 8, 768).transpose(2, 0, 1, 3).reshape(256, 768)
    parts = jnp.einsum("mk,zkn->zmn", attn, o_blocks, preferred_element_type=f32).astype(bf16)
    parts = exchange(parts.reshape(16, 32, WIDTH), SIDE)
    attended = jnp.sum(parts.astype(f32), axis=0)
    stream = x_in.astype(f32) + attended * o_scale

    squares = jnp.sum(stream * stream, axis=1, keepdims=True)
    high, low = high_low(squares)
    lane = lax.broadcasted_iota(jnp.int32, (32, 128), 1)
    extra = jnp.where(lane == 0, high, jnp.where(lane == 1, low, jnp.zeros((), bf16)))
    gained = jnp.concatenate([(stream * ffn_gain).astype(bf16), extra], axis=1)
    gained = spread(gained, SIDE, 16).reshape(2, 256, WIDTH + 128)
    weights = gate_up_blocks[:, : 2 * WIDTH].reshape(2, 2, WIDTH, UNITS)
    partial_value = jnp.einsum(
        "zmd,zkdf->mkf", gained[:, :, :WIDTH], weights, preferred_element_type=f32
    )
    block_squares = jnp.sum(gained[:, :, WIDTH:].astype(f32), axis=(0, 2), keepdims=False)[:, None]
    high, low = high_low(block_squares)
    lane = lax.broadcasted_iota(jnp.int32, (256, 128), 1)
    extra = jnp.where(lane == 0, high, jnp.where(lane == 1, low, jnp.zeros((), bf16)))
    partial_value = jnp.concatenate(
        [partial_value.reshape(256, 2 * UNITS).astype(bf16), extra], axis=1
    )
    shares = exchange(partial_value.reshape(16, 16, 2 * UNITS + 128), "b")
    shares = jnp.sum(shares.astype(f32), axis=0)
    squares = jnp.sum(shares[:, 2 * UNITS :], axis=1, keepdims=True)
    inverse = lax.rsqrt(squares / D + 1e-05)
    scales = gate_up_blocks[0, 2 * WIDTH : 2 * WIDTH + 4].astype(f32)
    scales = scales[:2] + scales[2:]
    gate_part = shares[:, :UNITS] * inverse * scales[0]
    up_part = shares[:, UNITS : 2 * UNITS] * inverse * scales[1]
    hidden = (jax.nn.silu(gate_part) * up_part).astype(bf16)
    hidden = spread(hidden, "b", 16).reshape(256, UNITS)
    parts = jnp.einsum("mk,zkn->zmn", hidden, down_blocks, preferred_element_type=f32).astype(bf16)
    parts = exchange(parts.reshape(16, 32, WIDTH), SIDE)
    lowered = jnp.sum(parts.astype(f32), axis=0)
    return (stream + lowered * down_scale).astype(bf16)


def solution(mesh):
    mesh = Mesh(mesh.devices.reshape(2, 4, 2, 16, 2), ("ylo", "x", "core", "b", "zl"))
    everywhere = ROWS + COLS
    in_specs = (
        P(ROWS, COLS),
        P(everywhere, None),
        P(everywhere, None, None),
        P(everywhere, None, None, None),
        P(everywhere),
        P(ROWS, COLS),
        P(COLS),
        P(COLS),
        P(None, COLS, ROWS),
        P(None, ROWS),
        P(ROWS, COLS),
        P(COLS),
    )
    out_specs = P(ROWS, COLS)
    return jax.shard_map(body, mesh=mesh, in_specs=in_specs, out_specs=out_specs, check_vma=False)
```

time: 671 us -> 210 us (0.31)
  waiting for transfers between devices: 408 us -> 68.4 us
  blocking collectives: 224 us -> 39.6 us
  starting transfers between devices: 0.13 us -> 53.3 us
  local copies, waits for them, and re-layouts: 3.82 us -> 13.9 us
    reduce_scatter x3 -> x0, waiting for transfers between devices: 326 us -> none  [the longest x1 206 us: body(): lax.psum_scatter(partial_value.astype(jnp.bfloat16), 'col', scatter_dimen...]
    all_gather x2 -> x0, blocking collectives: 122 us -> none  [the longest x1 87.7 us: body(): collected = lax.all_gather(attn_local, 'col', axis=0, tiled=True)]
    all_gather x1 -> x3, waiting for transfers between devices: 82.3 us -> 6.75 us  [both(): return lax.all_gather(block, 'core', axis=0, tiled=False)]
    psum x1 -> x0, blocking collectives: 68.9 us -> none  [body(): squares = lax.psum(jnp.sum(stream * stream, axis=1), 'col')]
    all_to_all x0 -> x4, starting transfers between devices: none -> 40.3 us  [exchange(): return lax.all_to_all(parts, axis, split_axis=0, concat_axis=0, tiled=False)]
    ppermute x0 -> x3, waiting for transfers between devices: none -> 33.4 us  [swap(): return lax.ppermute(block, ('core', 'zl'), [(0, 0), (1, 2), (2, 1), (3, 3)])]
    all_to_all x0 -> x4, waiting for transfers between devices: none -> 28.2 us  [exchange(): return lax.all_to_all(parts, axis, split_axis=0, concat_axis=0, tiled=False)]
    ppermute x0 -> x3, starting transfers between devices: none -> 12.8 us  [swap(): return lax.ppermute(block, ('core', 'zl'), [(0, 0), (1, 2), (2, 1), (3, 3)])]
  transfers between devices with their start and end apart: 4 -> 10, of which waited for: 4 -> 5; matrix products, arithmetic and copies ran while one was open for 0% -> 7% of each run, Pallas kernels for 0% -> 0%
where the time goes in v1:
time: 210 us; the launch traced here: 207 us
  waiting for transfers between devices  68.4 us (33%)
  starting transfers between devices  53.3 us (25%)
  blocking collectives  39.6 us (19%)
  between operations  14.1 us (7%)
  local copies, waits for them, and re-layouts  13.9 us (7%)
  other arithmetic  9.01 us (4%)
  matrix products  8.61 us (4%)
    all_to_all x4, starting transfers between devices, exchange(): return lax.all_to_all(parts, axis, split_axis=0, concat_axis=0, tiled=False)  40.3 us
    all_to_all x3, blocking collectives, exchange(): return lax.all_to_all(parts, axis, split_axis=0, concat_axis=0, tiled=False)  39.6 us
    ppermute x3, waiting for transfers between devices, swap(): return lax.ppermute(block, ('core', 'zl'), [(0, 0), (1, 2), (2, 1), (3, 3)])  33.4 us
    all_to_all x4, waiting for transfers between devices, exchange(): return lax.all_to_all(parts, axis, split_axis=0, concat_axis=0, tiled=False)  28.2 us
    ppermute x3, starting transfers between devices, swap(): return lax.ppermute(block, ('core', 'zl'), [(0, 0), (1, 2), (2, 1), (3, 3)])  12.8 us
    all_gather x3, waiting for transfers between devices, both(): return lax.all_gather(block, 'core', axis=0, tiled=False)  6.75 us
  transfers between devices with their start and end apart: 10, of which 5 were waited for; matrix products, arithmetic and copies ran while one was open for 7% of the time, Pallas kernels for 0%

profile of v1, /device:TPU:1, one launch (start us, length us, event | category | flops | bytes accessed | tf_op | source)
XLA Modules:
  0.0 206.8 jit_solution(1015116859920145070)
XLA Ops:
  6.5 5.5 %collective-permute-start = (bf16[768,384]{1,0:T(8,128)(2,1)}, bf16[768,384]{1,0:T(8,128)(2,1)}, u32[]{:S(2)}, u32[]{:S(2)}) collective-permute-start(bf16[768,384]{1,0:T(8,128)(2,1)} %param.17), channel_id=1, source_target_pairs={{0,0},{1,32},{32,1},{33,33},{2,2},{3,34},{34,3},{35,35},{4,4},{5,3... | collective-permute-start | bytes 1769480 | tf_op jit(solution)/shard_map/ppermute | solution.py:62
  12.1 0.8 subtract_convert_fusion
  12.9 3.1 %maximum_maximum_fusion = bf16[784,1152]{1,0:T(8,128)(2,1)} fusion(bf16[2,1152]{1,0:T(2,128)(2,1)S(1)} %get-tuple-element.7, bf16[2,1152]{1,0:T(2,128)(2,1)S(1)} %get-tuple-element.8, bf16[768,1152]{1,0:T(8,128)(2,1)} %bitcast.57, bf16[784]{0:T(1024)(128)(2,1)S(1)} %pad.5.clone), kind=kLoop, calls=%fused_computation.3 | loop fusion | flops 7225344 | bytes 3586592 | tf_op jit(solution)/shard_map/concatenate | solution.py:98
  16.0 2.0 collective-permute-start.1
  18.2 1.3 fusion.16
  22.1 0.7 reduce.9
  22.8 16.0 %all_to_all.39 = bf16[16,2,384]{2,1,0:T(2,128)(2,1)S(1)} all-to-all(bf16[16,2,384]{2,1,0:T(2,128)(2,1)S(1)} %reshape.196), channel_id=1, replica_groups=mesh['ylo'=2,'x'=4,'core'=2,'b'=16,'zl'=2] {'zl','ylo','x'}, dimensions={0} | all-to-all | bytes 49152 | tf_op jit(solution)/shard_map/all_to_all | solution.py:70
  38.8 0.8 broadcast_in_dim.91
  39.5 14.5 %all-to-all-start.1 = ((bf16[16,16,768]{2,1,0:T(8,128)(2,1)}), bf16[16,16,768]{2,1,0:T(8,128)(2,1)S(1)}, u32[]{:S(2)}, u32[]{:S(2)}) async-start(bf16[16,16,768]{2,1,0:T(8,128)(2,1)} %broadcast_in_dim.91), calls=%async_computation.1 | async-start | bytes 786432 | tf_op jit(solution)/shard_map/all_to_all | solution.py:70
  54.1 1.2 copy-done
  55.4 11.8 %all-to-all-done.1 = bf16[16,16,768]{2,1,0:T(8,128)(2,1)S(1)} async-done(((bf16[16,16,768]{2,1,0:T(8,128)(2,1)}), bf16[16,16,768]{2,1,0:T(8,128)(2,1)S(1)}, u32[]{:S(2)}, u32[]{:S(2)}) %all-to-all-start.1) | async-done | bytes 393248 | tf_op jit(solution)/shard_map/all_to_all | solution.py:70
  67.7 2.5 %convolution_convert_fusion.1 = bf16[256,2,384]{2,0,1:T(8,128)(2,1)} fusion(bf16[256,768,1]{1,0,2:T(8,128)(2,1)S(1)} %reshape.188, bf16[2,768,384]{2,1,0:T(8,128)(2,1)} %bitcast.59), kind=kOutput, calls=%fused_computation.5 | convolution fusion | flops 302186496 | bytes 1966080 | tf_op jit(solution)/shard_map/mk,zkn->zmn/dot_general | solution.py:116
  70.2 11.1 %all-to-all-start.2 = ((bf16[16,32,384]{2,1,0:T(8,128)(2,1)}), bf16[16,32,384]{2,1,0:T(8,128)(2,1)S(1)}, u32[]{:S(2)}, u32[]{:S(2)}) async-start(bf16[16,32,384]{2,1,0:T(8,128)(2,1)} %bitcast.13), calls=%async_computation.2 | async-start | bytes 786432 | tf_op jit(solution)/shard_map/all_to_all | solution.py:70
  81.3 8.5 %all-to-all-done.2 = bf16[16,32,384]{2,1,0:T(8,128)(2,1)S(1)} async-done(((bf16[16,32,384]{2,1,0:T(8,128)(2,1)}), bf16[16,32,384]{2,1,0:T(8,128)(2,1)S(1)}, u32[]{:S(2)}, u32[]{:S(2)}) %all-to-all-start.2) | async-done | bytes 393248 | tf_op jit(solution)/shard_map/all_to_all | solution.py:70
  90.5 11.5 %all_to_all.40 = bf16[16,32,512]{2,1,0:T(8,128)(2,1)S(1)} all-to-all(bf16[16,32,512]{2,1,0:T(8,128)(2,1)S(1)} %broadcast_in_dim.95), channel_id=1, replica_groups=mesh['ylo'=2,'x'=4,'core'=2,'b'=16,'zl'=2] {'zl','ylo','x'}, dimensions={0} | all-to-all | bytes 1048576 | tf_op jit(solution)/shard_map/all_to_all | solution.py:70
  102.0 0.8 copy-done.2
  103.0 0.8 select_select_fusion
  103.7 2.3 %slice.65 = bf16[2,768,1152]{2,1,0:T(8,128)(2,1)S(1)} slice(bf16[2,784,1152]{2,1,0:T(8,128)(2,1)} %bitcast.54), slice={[0:2], [0:768], [0:1152]} | slice | bytes 7077888 | tf_op jit(solution)/shard_map/slice | solution.py:127
  106.0 3.7 %copy.27 = bf16[2,1152,384,2]{2,1,0,3:T(8,128)(2,1)} copy(bf16[2,1152,384,2]{1,2,0,3:T(8,128)(2,1)S(1)} %bitcast.52) | data formatting | bytes 7077888 | tf_op jit(solution)/shard_map/zmd,zkdf->mkf/dot_general | solution.py:128
  109.7 3.3 %fusion = bf16[256,2304]{1,0:T(8,128)(2,1)S(1)} fusion(bf16[2304,384,2]{1,0,2:T(8,128)(2,1)} %bitcast.53, bf16[2,256,512]{2,1,0:T(8,128)(2,1)} %bitcast.61), kind=kOutput, calls=%fused_computation.1 | convolution fusion | flops 906559488 | bytes 5111808 | tf_op jit(solution)/shard_map/zmd,zkdf->mkf/dot_general | solution.py:128
  113.0 1.2 pad_maximum_fusion
  114.1 4.3 %all-to-all-start.4 = ((bf16[16,16,2432]{2,1,0:T(8,128)(2,1)}), bf16[16,16,2432]{2,1,0:T(8,128)(2,1)S(1)}, u32[]{:S(2)}, u32[]{:S(2)}) async-start(bf16[16,16,2432]{2,1,0:T(8,128)(2,1)} %bitcast.21), calls=%async_computation.4 | async-start | bytes 2490368 | tf_op jit(solution)/shard_map/all_to_all | solution.py:70
  118.5 5.3 %collective-permute-start.2 = (bf16[1152,384]{1,0:T(8,128)(2,1)S(1)}, bf16[1152,384]{1,0:T(8,128)(2,1)S(1)}, u32[]{:S(2)}, u32[]{:S(2)}) collective-permute-start(bf16[1152,384]{1,0:T(8,128)(2,1)S(1)} %copy-done.13), channel_id=1, source_target_pairs={{0,0},{1,32},{32,1},{33,33},{2,2},{3,34},{34,3},{35,35},{4,4},{5,3... | collective-permute-start | bytes 2654216 | tf_op jit(solution)/shard_map/ppermute | solution.py:62
  123.8 33.4 %collective-permute-done.2 = bf16[1152,384]{1,0:T(8,128)(2,1)S(1)} collective-permute-done((bf16[1152,384]{1,0:T(8,128)(2,1)S(1)}, bf16[1152,384]{1,0:T(8,128)(2,1)S(1)}, u32[]{:S(2)}, u32[]{:S(2)}) %collective-permute-start.2) | collective-permute-done | bytes 884768 | tf_op jit(solution)/shard_map/ppermute | solution.py:62
  157.2 0.9 copy-done.1
  158.1 0.7 slice_convert_fusion
  159.3 0.9 broadcast_in_dim.100
  160.2 10.4 %all-to-all-start.5 = ((bf16[16,16,1152]{2,1,0:T(8,128)(2,1)}), bf16[16,16,1152]{2,1,0:T(8,128)(2,1)S(1)}, u32[]{:S(2)}, u32[]{:S(2)}) async-start(bf16[16,16,1152]{2,1,0:T(8,128)(2,1)} %broadcast_in_dim.100), calls=%async_computation.5 | async-start | bytes 1179648 | tf_op jit(solution)/shard_map/all_to_all | solution.py:70
  170.7 6.7 %all-gather.11.cloned.1.call-done = bf16[2304,384]{1,0:T(8,128)(2,1)} async-done(((bf16[1152,384]{1,0:T(8,128)(2,1)}), bf16[2304,384]{1,0:T(8,128)(2,1)}) %all-gather.11.cloned.1.call-update) | async-done | bytes 1769488 | tf_op jit(solution)/shard_map/all_gather | solution.py:66
  177.4 7.9 %all-to-all-done.5 = bf16[16,16,1152]{2,1,0:T(8,128)(2,1)S(1)} async-done(((bf16[16,16,1152]{2,1,0:T(8,128)(2,1)}), bf16[16,16,1152]{2,1,0:T(8,128)(2,1)S(1)}, u32[]{:S(2)}, u32[]{:S(2)}) %all-to-all-start.5) | async-done | bytes 589856 | tf_op jit(solution)/shard_map/all_to_all | solution.py:70
  185.3 2.2 %convolution_convert_fusion = bf16[256,2,384]{2,0,1:T(8,128)(2,1)S(1)} fusion(bf16[256,1152,1]{1,0,2:T(8,128)(2,1)S(1)} %bitcast.62, bf16[2,1152,384]{2,1,0:T(8,128)(2,1)} %bitcast.71), kind=kOutput, calls=%fused_computation.4 | convolution fusion | flops 453181440 | bytes 2752512 | tf_op jit(solution)/shard_map/mk,zkn->zmn/dot_general | solution.py:148
  187.5 12.1 %all_to_all.41 = bf16[16,32,384]{2,1,0:T(8,128)(2,1)S(1)} all-to-all(bf16[16,32,384]{2,1,0:T(8,128)(2,1)S(1)} %bitcast.64), channel_id=1, replica_groups=mesh['ylo'=2,'x'=4,'core'=2,'b'=16,'zl'=2] {'zl','ylo','x'}, dimensions={0} | all-to-all | bytes 786432 | tf_op jit(solution)/shard_map/all_to_all | solution.py:70
  (75 shorter events, 4.8 us)
Async XLA Ops:
  6.5 11.5 %copy-start.8 = (bf16[1,12288]{1,0:T(2,128)(2,1)S(1)}, bf16[1,12288]{1,0:T(2,128)(2,1)}, u32[]{:S(2)}) copy-start(bf16[1,12288]{1,0:T(2,128)(2,1)} %param.13) | copy-start | bytes 73732
  6.5 61.1 %all-gather.7.cloned.1.call-start = ((), (), s32[]{:S(2)}) async-start(), calls=%async_computation.7 | async-start | bytes 1769472 | tf_op jit(solution)/shard_map/all_gather | solution.py:66
  6.5 14.3 %collective-permute-start = (bf16[768,384]{1,0:T(8,128)(2,1)}, bf16[768,384]{1,0:T(8,128)(2,1)}, u32[]{:S(2)}, u32[]{:S(2)}) collective-permute-start(bf16[768,384]{1,0:T(8,128)(2,1)} %param.17), channel_id=1, source_target_pairs={{0,0},{1,32},{32,1},{33,33},{2,2},{3,34},{34,3},{35,35},{4,4},{5,3... | collective-permute-start | bytes 1769480 | tf_op jit(solution)/shard_map/ppermute | solution.py:62
  16.0 3.5 %copy-start.10 = (bf16[1,2,1024]{2,1,0:T(2,128)(2,1)S(1)}, bf16[1,2,1024]{2,1,0:T(2,128)(2,1)}, u32[]{:S(2)}) copy-start(bf16[1,2,1024]{2,1,0:T(2,128)(2,1)} %param.14) | copy-start | bytes 12292
  16.0 38.1 %collective-permute-start.1 = (bf16[784,1152]{1,0:T(8,128)(2,1)}, bf16[784,1152]{1,0:T(8,128)(2,1)S(1)}, u32[]{:S(2)}, u32[]{:S(2)}) collective-permute-start(bf16[784,1152]{1,0:T(8,128)(2,1)} %maximum_maximum_fusion), channel_id=1, source_target_pairs={{0,0},{1,32},{32,1},{33,33},{2,2},{3,34},{34,3},{35,35},{4,4},{5,3... | collective-permute-start | bytes 5419016 | tf_op jit(solution)/shard_map/ppermute | solution.py:62
  39.5 27.6 %all-to-all-start.1 = ((bf16[16,16,768]{2,1,0:T(8,128)(2,1)}), bf16[16,16,768]{2,1,0:T(8,128)(2,1)S(1)}, u32[]{:S(2)}, u32[]{:S(2)}) async-start(bf16[16,16,768]{2,1,0:T(8,128)(2,1)} %broadcast_in_dim.91), calls=%async_computation.1 | async-start | bytes 786432 | tf_op jit(solution)/shard_map/all_to_all | solution.py:70
  54.0 49.7 %all-gather.9.cloned.1.call-start = ((), (), s32[]{:S(2)}) async-start(), calls=%async_computation.8 | async-start | bytes 5419008 | tf_op jit(solution)/shard_map/all_gather | solution.py:66
  54.1 1.2 copy-start
  67.4 22.4 %copy-start.6 = (bf16[32,384]{1,0:T(8,128)(2,1)S(1)}, bf16[32,384]{1,0:T(8,128)(2,1)}, u32[]{:S(2)}) copy-start(bf16[32,384]{1,0:T(8,128)(2,1)} %param.12) | copy-start | bytes 73732
  67.4 22.4 %copy-start.9 = (f32[384]{0:T(512)S(1)}, f32[384]{0:T(512)}, u32[]{:S(2)}) copy-start(f32[384]{0:T(512)} %param.18) | copy-start | bytes 4612
  67.5 22.4 %copy-start.12 = (f32[384]{0:T(512)S(1)}, f32[384]{0:T(512)}, u32[]{:S(2)}) copy-start(f32[384]{0:T(512)} %param.19) | copy-start | bytes 4612
  70.2 19.6 %all-to-all-start.2 = ((bf16[16,32,384]{2,1,0:T(8,128)(2,1)}), bf16[16,32,384]{2,1,0:T(8,128)(2,1)S(1)}, u32[]{:S(2)}, u32[]{:S(2)}) async-start(bf16[16,32,384]{2,1,0:T(8,128)(2,1)} %bitcast.13), calls=%async_computation.2 | async-start | bytes 786432 | tf_op jit(solution)/shard_map/all_to_all | solution.py:70
  89.8 0.6 copy-start.3
  102.0 0.8 copy-start.2
  109.7 3.3 %copy-start.5 = (bf16[256,128]{1,0:T(8,128)(2,1)S(1)}, bf16[256,128]{1,0:T(8,128)(2,1)}, u32[]{:S(2)}) copy-start(bf16[256,128]{1,0:T(8,128)(2,1)} %select_select_fusion) | copy-start | bytes 196612
  114.1 4.4 %copy-start.13 = (bf16[1152,384]{1,0:T(8,128)(2,1)S(1)}, bf16[1152,384]{1,0:T(8,128)(2,1)}, u32[]{:S(2)}) copy-start(bf16[1152,384]{1,0:T(8,128)(2,1)} %param.22) | copy-start | bytes 2654212
  114.1 44.8 %all-to-all-start.4 = ((bf16[16,16,2432]{2,1,0:T(8,128)(2,1)}), bf16[16,16,2432]{2,1,0:T(8,128)(2,1)S(1)}, u32[]{:S(2)}, u32[]{:S(2)}) async-start(bf16[16,16,2432]{2,1,0:T(8,128)(2,1)} %bitcast.21), calls=%async_computation.4 | async-start | bytes 2490368 | tf_op jit(solution)/shard_map/all_to_all | solution.py:70
  118.5 59.0 %all-gather.11.cloned.1.call-start = ((), (), s32[]{:S(2)}) async-start(), calls=%async_computation.9 | async-start | bytes 2654208 | tf_op jit(solution)/shard_map/all_gather | solution.py:66
  118.5 38.7 %collective-permute-start.2 = (bf16[1152,384]{1,0:T(8,128)(2,1)S(1)}, bf16[1152,384]{1,0:T(8,128)(2,1)S(1)}, u32[]{:S(2)}, u32[]{:S(2)}) collective-permute-start(bf16[1152,384]{1,0:T(8,128)(2,1)S(1)} %copy-done.13), channel_id=1, source_target_pairs={{0,0},{1,32},{32,1},{33,33},{2,2},{3,34},{34,3},{35,35},{4,4},{5,3... | collective-permute-start | bytes 2654216 | tf_op jit(solution)/shard_map/ppermute | solution.py:62
  157.2 0.9 copy-start.1
  160.2 25.1 %all-to-all-start.5 = ((bf16[16,16,1152]{2,1,0:T(8,128)(2,1)}), bf16[16,16,1152]{2,1,0:T(8,128)(2,1)S(1)}, u32[]{:S(2)}, u32[]{:S(2)}) async-start(bf16[16,16,1152]{2,1,0:T(8,128)(2,1)} %broadcast_in_dim.100), calls=%async_computation.5 | async-start | bytes 1179648 | tf_op jit(solution)/shard_map/all_to_all | solution.py:70
  185.3 14.3 %copy-start.4 = (f32[32,384]{1,0:T(8,128)S(1)}, f32[32,384]{1,0:T(8,128)}, u32[]{:S(2)}) copy-start(f32[32,384]{1,0:T(8,128)} %copy-done.3) | copy-start | bytes 147460
  185.3 14.3 %copy-start.7 = (bf16[32,384]{1,0:T(8,128)(2,1)S(1)}, bf16[32,384]{1,0:T(8,128)(2,1)}, u32[]{:S(2)}) copy-start(bf16[32,384]{1,0:T(8,128)(2,1)} %param.12) | copy-start | bytes 73732
  185.3 14.3 %copy-start.11 = (f32[384]{0:T(512)S(1)}, f32[384]{0:T(512)}, u32[]{:S(2)}) copy-start(f32[384]{0:T(512)} %param.23) | copy-start | bytes 4612
Sparse Core Ops, SparseCore 0:
  21.0 25.0 all-gather.6
  57.0 26.4 all-gather.8
  158.3 19.1 all-gather.10

commit v2 on v1

v2 whole, which is shorter than its diff:
```python
import jax
import jax.numpy as jnp
from jax import lax
from jax.experimental import pallas as pl
from jax.experimental.pallas import tpu as pltpu
from jax.sharding import Mesh
from jax.sharding import PartitionSpec as P

D = 12288
GROUPS = 8
GROUP_HEADS = 12
HEAD_SIZE = 128
CONTEXT_SLOTS = 256
UNITS = 1152
WIDTH = 384
EXTRA = 128
PACK_SCALES = 768
PACK_ROWS = 784

ROWS = ("ylo", "x", "core")
COLS = ("b", "zl")
NEAR = ("ylo", "x")
SIDE = ("zl", "ylo", "x")
bf16 = jnp.bfloat16
f32 = jnp.float32

VMEM = pl.BlockSpec(memory_space=pltpu.VMEM)
SMEM = pl.BlockSpec(memory_space=pltpu.SMEM)
HBM = pl.BlockSpec(memory_space=pltpu.HBM)
PARAMS = pltpu.CompilerParams(vmem_limit_bytes=32 * 1024 * 1024)


def dot(a, b):
    return jnp.dot(a, b, preferred_element_type=f32)


def high_low(value):
    high = value.astype(bf16).astype(f32)
    return high, value - high


def in_hbm(array):
    return pltpu.with_memory_space_constraint(array, pltpu.HBM)


def pack_kernel(weight_ref, scale_ref, gain_ref, out_ref, scale, gain, sems):
    copies = [
        pltpu.make_async_copy(scale_ref, scale, sems.at[0]),
        pltpu.make_async_copy(gain_ref, gain, sems.at[1]),
        pltpu.make_async_copy(weight_ref, out_ref.at[pl.ds(0, PACK_SCALES), :], sems.at[2]),
    ]
    for copy in copies:
        copy.start()
    copies[0].wait()
    copies[1].wait()
    rows = [
        part[k : k + 1, j * WIDTH : (j + 1) * WIDTH]
        for part in high_low(scale[...])
        for k in range(2)
        for j in range(3)
    ]
    rows.extend(high_low(gain[...].reshape(1, WIDTH)))
    rows.append(jnp.zeros((2, WIDTH), f32))
    out_ref[PACK_SCALES:, :] = jnp.concatenate(rows, axis=0).astype(bf16)
    copies[2].wait()


def pack(o_weight, gate_up_scale, ffn_gain):
    return pl.pallas_call(
        pack_kernel,
        out_shape=jax.ShapeDtypeStruct((PACK_ROWS, WIDTH), bf16),
        in_specs=[HBM, HBM, HBM],
        out_specs=VMEM,
        scratch_shapes=[
            pltpu.VMEM((2, UNITS), f32),
            pltpu.VMEM((WIDTH,), f32),
            pltpu.SemaphoreType.DMA((3,)),
        ],
        compiler_params=PARAMS,
        name="pack",
    )(in_hbm(o_weight), in_hbm(gate_up_scale), in_hbm(ffn_gain))


def attend_kernel(
    length_ref, query_in, latest_in, cache_ref, out_ref, query_row, latest_ref, query_ref, cache, sems
):
    small = [
        pltpu.make_async_copy(query_in, query_row, sems.at[2]),
        pltpu.make_async_copy(latest_in, latest_ref, sems.at[3]),
    ]
    for copy in small:
        copy.start()
    copies = [
        pltpu.make_async_copy(cache_ref.at[0, part], cache.at[part], sems.at[part])
        for part in range(2)
    ]
    for copy in copies:
        copy.start()
    for copy in small:
        copy.wait()
    for g in range(GROUPS):
        for h in range(GROUP_HEADS):
            at = (g * GROUP_HEADS + h) * HEAD_SIZE
            query_ref[g, h : h + 1] = query_row[:, at : at + HEAD_SIZE].astype(f32)
    scale = HEAD_SIZE ** (-0.5)
    slot = lax.broadcasted_iota(jnp.int32, (GROUP_HEADS, CONTEXT_SLOTS), 1)
    valid = slot < length_ref[0]
    lanes = [slice(g * HEAD_SIZE, (g + 1) * HEAD_SIZE) for g in range(GROUPS)]
    fresh = [
        jnp.sum(
            query_ref[g] * latest_ref[0, 0:1, lanes[g]].astype(f32),
            axis=1,
            keepdims=True,
        )
        * scale
        for g in range(GROUPS)
    ]
    copies[0].wait()
    cached = [
        jnp.where(
            valid,
            lax.dot_general(
                query_ref[g].astype(bf16),
                cache[0, :, lanes[g]],
                (((1,), (1,)), ((), ())),
                preferred_element_type=f32,
            )
            * scale,
            -jnp.inf,
        )
        for g in range(GROUPS)
    ]
    tops = [
        jnp.maximum(jnp.max(cached[g], axis=1, keepdims=True), fresh[g]) for g in range(GROUPS)
    ]
    weights = [jnp.exp(cached[g] - tops[g]) for g in range(GROUPS)]
    fresh = [jnp.exp(fresh[g] - tops[g]) for g in range(GROUPS)]
    inverse = [
        1.0 / (jnp.sum(weights[g], axis=1, keepdims=True) + fresh[g]) for g in range(GROUPS)
    ]
    probs = [(weights[g] * inverse[g]).astype(bf16) for g in range(GROUPS)]
    fresh = [(fresh[g] * inverse[g]).astype(bf16).astype(f32) for g in range(GROUPS)]
    copies[1].wait()
    mixed = [
        dot(probs[g], cache[1, :, lanes[g]])
        + fresh[g] * latest_ref[0, 1:2, lanes[g]].astype(f32)
        for g in range(GROUPS)
    ]
    for g in range(GROUPS):
        out_ref[g] = mixed[g].astype(bf16)


def attend(query, latest_key_value, key_value_cache, lengths):
    return pl.pallas_call(
        attend_kernel,
        out_shape=jax.ShapeDtypeStruct((GROUPS, GROUP_HEADS, HEAD_SIZE), bf16),
        in_specs=[SMEM, HBM, HBM, HBM],
        out_specs=VMEM,
        scratch_shapes=[
            pltpu.VMEM((1, D), bf16),
            pltpu.VMEM((1, 2, GROUPS * HEAD_SIZE), bf16),
            pltpu.VMEM((GROUPS, GROUP_HEADS, HEAD_SIZE), f32),
            pltpu.VMEM((2, CONTEXT_SLOTS, GROUPS * HEAD_SIZE), bf16),
            pltpu.SemaphoreType.DMA((4,)),
        ],
        compiler_params=PARAMS,
        name="attend",
    )(lengths, in_hbm(query), in_hbm(latest_key_value), in_hbm(key_value_cache))


def repeat_kernel(heads_ref, out_ref):
    half = GROUP_HEADS // 2
    for z in range(2):
        for j in range(half):
            block = heads_ref[:, z * half + j, :]
            for b in range(16):
                out_ref[2 * b + z, :, j * HEAD_SIZE : (j + 1) * HEAD_SIZE] = block


def repeat(heads):
    return pl.pallas_call(
        repeat_kernel,
        out_shape=jax.ShapeDtypeStruct((32, 8, 768), bf16),
        in_specs=[VMEM],
        out_specs=VMEM,
        compiler_params=PARAMS,
        name="repeat",
    )(heads)


def project_kernel(attn_ref, weight_ref, out_ref, weight, sems):
    copies = [
        pltpu.make_async_copy(
            weight_ref.at[z, pl.ds(0, PACK_SCALES), :], weight.at[z], sems.at[z]
        )
        for z in range(2)
    ]
    for copy in copies:
        copy.start()
    row = lax.broadcasted_iota(jnp.int32, (256, 256), 0)
    source = (row & 31) * 8 + (row >> 5)
    pick = (lax.broadcasted_iota(jnp.int32, (256, 256), 1) == source).astype(f32).astype(bf16)
    attn = attn_ref[...].astype(f32).reshape(256, 768).astype(bf16)
    attn = dot(pick, attn).astype(bf16)
    for z in range(2):
        copies[z].wait()
        out_ref[z] = dot(attn, weight[z]).astype(bf16)


def project(attn, weights):
    return pl.pallas_call(
        project_kernel,
        out_shape=jax.ShapeDtypeStruct((2, 256, WIDTH), bf16),
        in_specs=[VMEM, HBM],
        out_specs=VMEM,
        scratch_shapes=[pltpu.VMEM((2, 768, WIDTH), bf16), pltpu.SemaphoreType.DMA((2,))],
        compiler_params=PARAMS,
        name="project",
    )(attn, in_hbm(weights))


def stream_kernel(parts_ref, x_ref, scale_ref, gain_ref, stream_ref, out_ref):
    attended = parts_ref[0].astype(f32)
    for s in range(1, 16):
        attended = attended + parts_ref[s].astype(f32)
    stream = x_ref[...].astype(f32) + attended * scale_ref[...]
    stream_ref[...] = stream
    gained = (stream * gain_ref[...]).astype(bf16)
    for s in range(16):
        out_ref[s] = gained


def stream_and_spread(parts, x_in, o_scale, ffn_gain):
    return pl.pallas_call(
        stream_kernel,
        out_shape=(
            jax.ShapeDtypeStruct((32, WIDTH), f32),
            jax.ShapeDtypeStruct((16, 32, WIDTH), bf16),
        ),
        in_specs=[VMEM] * 4,
        out_specs=(VMEM, VMEM),
        compiler_params=PARAMS,
        name="stream",
    )(parts, x_in, o_scale[None], ffn_gain[None])


def gate_up_kernel(rows_ref, weight_ref, packed_ref, out_ref, weight, scales, sems, scale_sem):
    copies = [
        pltpu.make_async_copy(
            weight_ref.at[z, pl.ds(k * WIDTH, WIDTH), :],
            weight.at[k, pl.ds(z * WIDTH, WIDTH), :],
            sems.at[k, z],
        )
        for k in range(2)
        for z in range(2)
    ]
    scale_copy = pltpu.make_async_copy(
        packed_ref.at[:, pl.ds(PACK_SCALES, 16), :], scales, scale_sem.at[0]
    )
    for copy in copies:
        copy.start()
    scale_copy.start()
    rows = [rows_ref[z * 8 : z * 8 + 8].reshape(256, WIDTH) for z in range(2)]
    both_rows = jnp.concatenate(rows, axis=1)
    for k in range(2):
        copies[2 * k].wait()
        copies[2 * k + 1].wait()
        for j in range(3):
            column = (k * 3 + j) * WIDTH
            out_ref[:, column : column + WIDTH] = dot(
                both_rows, weight[k, :, j * WIDTH : (j + 1) * WIDTH]
            ).astype(bf16)
    scale_copy.wait()
    squares = jnp.zeros((256, 1), f32)
    for z in range(2):
        gain = scales[z].astype(f32)
        gain = gain[12:13] + gain[13:14]
        scaled = rows[z].astype(f32) * (1.0 / gain)
        squares = squares + jnp.sum(scaled * scaled, axis=1, keepdims=True)
    high, low = high_low(squares)
    lane = lax.broadcasted_iota(jnp.int32, (256, EXTRA), 1)
    out_ref[:, 2 * UNITS :] = jnp.where(
        lane == 0, high, jnp.where(lane == 1, low, 0.0)
    ).astype(bf16)


def gate_up(rows, weights, packed):
    return pl.pallas_call(
        gate_up_kernel,
        out_shape=jax.ShapeDtypeStruct((256, 2 * UNITS + EXTRA), bf16),
        in_specs=[VMEM, HBM, HBM],
        out_specs=VMEM,
        scratch_shapes=[
            pltpu.VMEM((2, 2 * WIDTH, UNITS), bf16),
            pltpu.VMEM((2, 16, WIDTH), bf16),
            pltpu.SemaphoreType.DMA((2, 2)),
            pltpu.SemaphoreType.DMA((1,)),
        ],
        compiler_params=PARAMS,
        name="gate_up",
    )(rows, in_hbm(weights), in_hbm(packed))


def hidden_kernel(shares_ref, packed_ref, out_ref, scale_rows, sem):
    copy = pltpu.make_async_copy(
        packed_ref.at[0, pl.ds(PACK_SCALES, 16), :], scale_rows, sem.at[0]
    )
    copy.start()
    extra = shares_ref[0, :, 2 * UNITS :].astype(f32)
    for s in range(1, 16):
        extra = extra + shares_ref[s, :, 2 * UNITS :].astype(f32)
    squares = jnp.sum(extra, axis=1, keepdims=True)
    inverse = lax.rsqrt(squares / D + 1e-05)
    copy.wait()
    scales = scale_rows[...].astype(f32)
    scales = scales[0:6] + scales[6:12]
    for j in range(3):
        parts = []
        for k in range(2):
            lanes = slice((k * 3 + j) * WIDTH, (k * 3 + j + 1) * WIDTH)
            total = shares_ref[0, :, lanes].astype(f32)
            for s in range(1, 16):
                total = total + shares_ref[s, :, lanes].astype(f32)
            parts.append(total * inverse * scales[k * 3 + j : k * 3 + j + 1])
        gate, up = parts
        hidden = (gate / (1.0 + jnp.exp(-gate)) * up).astype(bf16)
        for b in range(16):
            out_ref[b, :, j * WIDTH : (j + 1) * WIDTH] = hidden


def hidden_and_spread(shares, packed):
    return pl.pallas_call(
        hidden_kernel,
        out_shape=jax.ShapeDtypeStruct((16, 16, UNITS), bf16),
        in_specs=[VMEM, HBM],
        out_specs=VMEM,
        scratch_shapes=[pltpu.VMEM((16, WIDTH), bf16), pltpu.SemaphoreType.DMA((1,))],
        compiler_params=PARAMS,
        name="hidden",
    )(shares, in_hbm(packed))


def down_kernel(hidden_ref, weight_ref, out_ref, weight, sems):
    copies = [
        pltpu.make_async_copy(weight_ref.at[z], weight.at[z], sems.at[z]) for z in range(2)
    ]
    for copy in copies:
        copy.start()
    hidden = hidden_ref[...].reshape(256, UNITS)
    for z in range(2):
        copies[z].wait()
        out_ref[z] = dot(hidden, weight[z]).astype(bf16)


def down(hidden, weights):
    return pl.pallas_call(
        down_kernel,
        out_shape=jax.ShapeDtypeStruct((2, 256, WIDTH), bf16),
        in_specs=[VMEM, HBM],
        out_specs=VMEM,
        scratch_shapes=[pltpu.VMEM((2, UNITS, WIDTH), bf16), pltpu.SemaphoreType.DMA((2,))],
        compiler_params=PARAMS,
        name="down",
    )(hidden, in_hbm(weights))


def swap(block):
    return lax.ppermute(block, ("core", "zl"), [(0, 0), (1, 2), (2, 1), (3, 3)])


def both(block):
    return lax.all_gather(block, "core", axis=0, tiled=False)


def exchange(parts, axis):
    return lax.all_to_all(parts, axis, split_axis=0, concat_axis=0, tiled=False)


def body(
    x_in,
    query,
    latest_key_value,
    key_value_cache,
    lengths,
    o_weight,
    o_scale,
    ffn_gain,
    gate_up_weight,
    gate_up_scale,
    down_weight,
    down_scale,
):
    packed = swap(pack(o_weight, gate_up_scale, ffn_gain))
    gate_up_weight = swap(gate_up_weight.reshape(2 * WIDTH, UNITS))
    heads = attend(query, latest_key_value, key_value_cache, lengths)
    heads = exchange(heads, NEAR)
    heads, packed = lax.optimization_barrier((heads, packed))
    packed = both(packed)
    attn = exchange(repeat(heads), COLS)
    attn, gate_up_weight, down_weight = lax.optimization_barrier(
        (attn, gate_up_weight, down_weight)
    )
    gate_up_weight = both(gate_up_weight)
    down_weight = swap(down_weight)
    parts = exchange(project(attn, packed).reshape(16, 32, WIDTH), SIDE)
    stream, rows = stream_and_spread(parts, x_in, o_scale, ffn_gain)
    rows = exchange(rows, SIDE)
    rows, down_weight = lax.optimization_barrier((rows, down_weight))
    down_weight = both(down_weight)
    shares = exchange(
        gate_up(rows, gate_up_weight, packed).reshape(16, 16, 2 * UNITS + EXTRA), "b"
    )
    hidden = hidden_and_spread(shares, packed)
    hidden = exchange(hidden, "b")
    parts = exchange(down(hidden, down_weight).reshape(16, 32, WIDTH), SIDE)
    lowered = jnp.sum(parts.astype(f32), axis=0)
    return (stream + lowered * down_scale).astype(bf16)


def solution(mesh):
    mesh = Mesh(mesh.devices.reshape(2, 4, 2, 16, 2), ("ylo", "x", "core", "b", "zl"))
    everywhere = ROWS + COLS
    in_specs = (
        P(ROWS, COLS),
        P(everywhere, None),
        P(everywhere, None, None),
        P(everywhere, None, None, None),
        P(everywhere),
        P(ROWS, COLS),
        P(COLS),
        P(COLS),
        P(None, COLS, ROWS),
        P(None, ROWS),
        P(ROWS, COLS),
        P(COLS),
    )
    out_specs = P(ROWS, COLS)
    return jax.shard_map(body, mesh=mesh, in_specs=in_specs, out_specs=out_specs, check_vma=False)
```

time: 210 us -> 188 us (0.90)
  starting transfers between devices: 53.3 us -> 35.2 us
  Pallas kernels: 0 us -> 14.7 us
  blocking collectives: 39.6 us -> 52.3 us
  local copies, waits for them, and re-layouts: 13.9 us -> 2.09 us
  matrix products: 8.61 us -> 0 us
  other arithmetic: 9.01 us -> 0.68 us
    all_to_all x4, waiting for transfers between devices: 28.2 us -> 60.8 us  [exchange(): return lax.all_to_all(parts, axis, split_axis=0, concat_axis=0, tiled=False)]
    ppermute x3, waiting for transfers between devices: 33.4 us -> 6.39 us  [swap(): return lax.ppermute(block, ('core', 'zl'), [(0, 0), (1, 2), (2, 1), (3, 3)])]
    all_to_all x4, starting transfers between devices: 40.3 us -> 22.6 us  [exchange(): return lax.all_to_all(parts, axis, split_axis=0, concat_axis=0, tiled=False)]
    pallas_call x0 -> x8, Pallas kernels: none -> 14.7 us  [the longest x1 4.3 us: gate_up(): pl.pallas_call(gate_up_kernel, out_shape=jax.ShapeDtypeStruct((256, 2 * U...]
    all_to_all x3, blocking collectives: 39.6 us -> 52.3 us  [exchange(): return lax.all_to_all(parts, axis, split_axis=0, concat_axis=0, tiled=False)]
    dot_general x6 -> x0, matrix products: 8.61 us -> none  [the longest x1 3.27 us: body(): jnp.einsum('zmd,zkdf->mkf', gained[:, :, :WIDTH], weights, preferred_elem...]
    all_gather x3, waiting for transfers between devices: 6.75 us -> 0.04 us  [both(): return lax.all_gather(block, 'core', axis=0, tiled=False)]
    concatenate x3 -> x0, other arithmetic: 4.26 us -> none  [the longest x1 3.09 us: body(): jnp.concatenate([gate_up_weight.reshape(2 * WIDTH, UNITS), scale_high, sc...]
  transfers between devices with their start and end apart: 10 -> 10, of which waited for: 5 -> 5; matrix products, arithmetic and copies ran while one was open for 7% -> 0% of each run, Pallas kernels for 0% -> 4%
where the time goes in v2:
time: 188 us; the launch traced here: 187 us
  waiting for transfers between devices  67.9 us (36%)
  blocking collectives  52.3 us (28%)
  starting transfers between devices  35.2 us (19%)
  Pallas kernels  14.7 us (8%)
  between operations  14 us (7%)
  local copies, waits for them, and re-layouts  2.09 us (1%)
    all_to_all x4, waiting for transfers between devices, exchange(): return lax.all_to_all(parts, axis, split_axis=0, concat_axis=0, tiled=False)  60.8 us
    all_to_all x3, blocking collectives, exchange(): return lax.all_to_all(parts, axis, split_axis=0, concat_axis=0, tiled=False)  52.3 us
    all_to_all x4, starting transfers between devices, exchange(): return lax.all_to_all(parts, axis, split_axis=0, concat_axis=0, tiled=False)  22.6 us
    ppermute x3, starting transfers between devices, swap(): return lax.ppermute(block, ('core', 'zl'), [(0, 0), (1, 2), (2, 1), (3, 3)])  12.6 us
    ppermute x3, waiting for transfers between devices, swap(): return lax.ppermute(block, ('core', 'zl'), [(0, 0), (1, 2), (2, 1), (3, 3)])  6.39 us
    pallas_call x1, Pallas kernels, gate_up(): pl.pallas_call(gate_up_kernel, out_shape=jax.ShapeDtypeStruct((256, 2 * U...  4.3 us
  transfers between devices with their start and end apart: 10, of which 5 were waited for; matrix products, arithmetic and copies ran while one was open for 0% of the time, Pallas kernels for 4%

profile of v2, /device:TPU:1, one launch (start us, length us, event | category | flops | bytes accessed | tf_op | source)
XLA Modules:
  0.0 186.9 jit_solution(1467522486454007896)
XLA Ops:
  6.5 1.1 pack.1
  7.7 5.4 %collective-permute-start = (bf16[784,384]{1,0:T(8,128)(2,1)S(1)}, bf16[784,384]{1,0:T(8,128)(2,1)S(1)}, u32[]{:S(2)}, u32[]{:S(2)}) collective-permute-start(bf16[784,384]{1,0:T(8,128)(2,1)S(1)} %pack.1), channel_id=1, source_target_pairs={{0,0},{1,32},{32,1},{33,33},{2,2},{3,34},{34,3},{35,35},{4,4},{5,3... | collective-permute-start | bytes 1806344 | tf_op jit(solution)/shard_map/ppermute | solution.py:368
  13.1 1.9 %collective-permute-start.1 = (bf16[768,1152]{1,0:T(8,128)(2,1)}, bf16[768,1152]{1,0:T(8,128)(2,1)S(1)}, u32[]{:S(2)}, u32[]{:S(2)}) collective-permute-start(bf16[768,1152]{1,0:T(8,128)(2,1)} %bitcast.13), channel_id=1, source_target_pairs={{0,0},{1,32},{32,1},{33,33},{2,2},{3,34},{34,3},{35,35},{4,4},{5,3... | collective-permute-start | bytes 5308424 | tf_op jit(solution)/shard_map/ppermute | solution.py:368
  15.6 1.7 attend.1
  17.4 9.9 %all_to_all.35.heads_ref = bf16[8,12,128]{2,1,0:T(8,128)(2,1)S(1)} all-to-all(bf16[8,12,128]{2,1,0:T(8,128)(2,1)S(1)} %attend.1), channel_id=1, replica_groups=mesh['ylo'=2,'x'=4,'core'=2,'b'=16,'zl'=2] {'ylo','x'}, dimensions={0} | all-to-all | bytes 49152 | tf_op jit(solution)/shard_map/all_to_all | solution.py:376
  27.3 0.8 copy-done.3
  28.2 0.0 all-gather.9.cloned.1.call-start
  28.2 0.1 repeat.1
  28.3 27.5 %all_to_all.36.attn_ref = bf16[32,8,768]{2,1,0:T(8,128)(2,1)S(1)} all-to-all(bf16[32,8,768]{2,1,0:T(8,128)(2,1)S(1)} %repeat.1), channel_id=1, replica_groups=mesh['ylo'=2,'x'=4,'core'=2,'b'=16,'zl'=2] {'b','zl'}, dimensions={0} | all-to-all | bytes 786432 | tf_op jit(solution)/shard_map/all_to_all | solution.py:376
  55.8 1.2 copy-done.1
  57.1 0.0 all-gather.7.cloned.1.call-done
  57.2 2.7 %project.1 = bf16[2,256,384]{2,1,0:T(8,128)(2,1)} custom-call(bf16[32,8,768]{2,1,0:T(8,128)(2,1)S(1)} %all_to_all.36.attn_ref, bf16[2,784,384]{2,1,0:T(8,128)(2,1)} %bitcast.8), custom_call_target="tpu_custom_call" | custom-call | tf_op jit(solution)/shard_map/project/pallas_call | solution.py:211
  59.9 5.6 %all-to-all-start.2 = ((bf16[16,32,384]{2,1,0:T(8,128)(2,1)}), bf16[16,32,384]{2,1,0:T(8,128)(2,1)S(1)}, u32[]{:S(2)}, u32[]{:S(2)}) async-start(bf16[16,32,384]{2,1,0:T(8,128)(2,1)} %bitcast.2), calls=%async_computation.2 | async-start | bytes 786432 | tf_op jit(solution)/shard_map/all_to_all | solution.py:376
  65.6 5.3 %collective-permute-start.2 = (bf16[1152,384]{1,0:T(8,128)(2,1)S(1)}, bf16[1152,384]{1,0:T(8,128)(2,1)S(1)}, u32[]{:S(2)}, u32[]{:S(2)}) collective-permute-start(bf16[1152,384]{1,0:T(8,128)(2,1)S(1)} %copy-done.7), channel_id=1, source_target_pairs={{0,0},{1,32},{32,1},{33,33},{2,2},{3,34},{34,3},{35,35},{4,4},{5,3... | collective-permute-start | bytes 2654216 | tf_op jit(solution)/shard_map/ppermute | solution.py:368
  70.9 2.8 %all-to-all-done.2.parts_ref = bf16[16,32,384]{2,1,0:T(8,128)(2,1)S(1)} async-done(((bf16[16,32,384]{2,1,0:T(8,128)(2,1)}), bf16[16,32,384]{2,1,0:T(8,128)(2,1)S(1)}, u32[]{:S(2)}, u32[]{:S(2)}) %all-to-all-start.2) | async-done | bytes 393248 | tf_op jit(solution)/shard_map/all_to_all | solution.py:376
  73.7 0.8 stream.1
  74.5 3.6 %all-to-all-start.3 = ((bf16[16,32,384]{2,1,0:T(8,128)(2,1)}), bf16[16,32,384]{2,1,0:T(8,128)(2,1)S(1)}, u32[]{:S(2)}, u32[]{:S(2)}) async-start(bf16[16,32,384]{2,1,0:T(8,128)(2,1)} %get-tuple-element.18), calls=%async_computation.3 | async-start | bytes 786432 | tf_op jit(solution)/shard_map/all_to_all | solution.py:376
  78.1 6.4 %collective-permute-done.2 = bf16[1152,384]{1,0:T(8,128)(2,1)S(1)} collective-permute-done((bf16[1152,384]{1,0:T(8,128)(2,1)S(1)}, bf16[1152,384]{1,0:T(8,128)(2,1)S(1)}, u32[]{:S(2)}, u32[]{:S(2)}) %collective-permute-start.2) | collective-permute-done | bytes 884768 | tf_op jit(solution)/shard_map/ppermute | solution.py:368
  84.5 1.7 all-to-all-done.3.rows_ref
  86.1 4.3 %gate_up.1 = bf16[256,2432]{1,0:T(8,128)(2,1)} custom-call(bf16[16,32,384]{2,1,0:T(8,128)(2,1)S(1)} %all-to-all-done.3.rows_ref, bf16[2,768,1152]{2,1,0:T(8,128)(2,1)} %bitcast.11, bf16[2,784,384]{2,1,0:T(8,128)(2,1)} %bitcast.9), custom_call_target="tpu_custom_call" | custom-call | tf_op jit(solution)/shard_map/gate_up/pallas_call | solution.py:288
  90.4 8.1 %all-to-all-start.4 = ((bf16[16,16,2432]{2,1,0:T(8,128)(2,1)}), bf16[16,16,2432]{2,1,0:T(8,128)(2,1)S(1)}, u32[]{:S(2)}, u32[]{:S(2)}) async-start(bf16[16,16,2432]{2,1,0:T(8,128)(2,1)} %bitcast.4), calls=%async_computation.4 | async-start | bytes 2490368 | tf_op jit(solution)/shard_map/all_to_all | solution.py:376
  98.6 0.0 all-gather.11.cloned.1.call-start
  98.6 0.7 all-gather.11.cloned.1.call-update
  99.3 37.8 %all-to-all-done.4.shares_ref = bf16[16,16,2432]{2,1,0:T(8,128)(2,1)S(1)} async-done(((bf16[16,16,2432]{2,1,0:T(8,128)(2,1)}), bf16[16,16,2432]{2,1,0:T(8,128)(2,1)S(1)}, u32[]{:S(2)}, u32[]{:S(2)}) %all-to-all-start.4) | async-done | bytes 1245216 | tf_op jit(solution)/shard_map/all_to_all | solution.py:376
  137.1 1.8 hidden.1
  138.9 5.2 %all-to-all-start.5 = ((bf16[16,16,1152]{2,1,0:T(8,128)(2,1)}), bf16[16,16,1152]{2,1,0:T(8,128)(2,1)S(1)}, u32[]{:S(2)}, u32[]{:S(2)}) async-start(bf16[16,16,1152]{2,1,0:T(8,128)(2,1)} %hidden.1), calls=%async_computation.5 | async-start | bytes 1179648 | tf_op jit(solution)/shard_map/all_to_all | solution.py:376
  144.1 0.0 all-gather.11.cloned.1.call-done
  144.1 18.5 %all-to-all-done.5.hidden_ref = bf16[16,16,1152]{2,1,0:T(8,128)(2,1)S(1)} async-done(((bf16[16,16,1152]{2,1,0:T(8,128)(2,1)}), bf16[16,16,1152]{2,1,0:T(8,128)(2,1)S(1)}, u32[]{:S(2)}, u32[]{:S(2)}) %all-to-all-start.5) | async-done | bytes 589856 | tf_op jit(solution)/shard_map/all_to_all | solution.py:376
  162.6 2.2 %down.1 = bf16[2,256,384]{2,1,0:T(8,128)(2,1)S(1)} custom-call(bf16[16,16,1152]{2,1,0:T(8,128)(2,1)S(1)} %all-to-all-done.5.hidden_ref, bf16[2,1152,384]{2,1,0:T(8,128)(2,1)} %bitcast.12), custom_call_target="tpu_custom_call" | custom-call | tf_op jit(solution)/shard_map/down/pallas_call | solution.py:356
  164.9 14.8 %all_to_all.37 = bf16[16,32,384]{2,1,0:T(8,128)(2,1)S(1)} all-to-all(bf16[16,32,384]{2,1,0:T(8,128)(2,1)S(1)} %bitcast.7), channel_id=1, replica_groups=mesh['ylo'=2,'x'=4,'core'=2,'b'=16,'zl'=2] {'zl','ylo','x'}, dimensions={0} | all-to-all | bytes 786432 | tf_op jit(solution)/shard_map/all_to_all | solution.py:376
  179.7 0.1 convert_reduce_fusion
  179.7 0.6 add_convert_fusion
  (22 shorter events, 0.1 us)
Async XLA Ops:
  6.5 50.6 %all-gather.7.cloned.1.call-start = ((), (), s32[]{:S(2)}) async-start(), calls=%async_computation.7 | async-start | bytes 1806336 | tf_op jit(solution)/shard_map/all_gather | solution.py:372
  7.7 19.7 %collective-permute-start = (bf16[784,384]{1,0:T(8,128)(2,1)S(1)}, bf16[784,384]{1,0:T(8,128)(2,1)S(1)}, u32[]{:S(2)}, u32[]{:S(2)}) collective-permute-start(bf16[784,384]{1,0:T(8,128)(2,1)S(1)} %pack.1), channel_id=1, source_target_pairs={{0,0},{1,32},{32,1},{33,33},{2,2},{3,34},{34,3},{35,35},{4,4},{5,3... | collective-permute-start | bytes 1806344 | tf_op jit(solution)/shard_map/ppermute | solution.py:368
  13.1 42.8 %collective-permute-start.1 = (bf16[768,1152]{1,0:T(8,128)(2,1)}, bf16[768,1152]{1,0:T(8,128)(2,1)S(1)}, u32[]{:S(2)}, u32[]{:S(2)}) collective-permute-start(bf16[768,1152]{1,0:T(8,128)(2,1)} %bitcast.13), channel_id=1, source_target_pairs={{0,0},{1,32},{32,1},{33,33},{2,2},{3,34},{34,3},{35,35},{4,4},{5,3... | collective-permute-start | bytes 5308424 | tf_op jit(solution)/shard_map/ppermute | solution.py:368
  27.3 0.8 copy-start.3
  28.2 57.9 %all-gather.9.cloned.1.call-start = ((), (), s32[]{:S(2)}) async-start(), calls=%async_computation.8 | async-start | bytes 5308416 | tf_op jit(solution)/shard_map/all_gather | solution.py:372
  55.8 1.2 copy-start.1
  57.1 8.5 %copy-start.7 = (bf16[1152,384]{1,0:T(8,128)(2,1)S(1)}, bf16[1152,384]{1,0:T(8,128)(2,1)}, u32[]{:S(2)}) copy-start(bf16[1152,384]{1,0:T(8,128)(2,1)} %param.22) | copy-start | bytes 2654212
  57.1 13.7 %copy-start.4 = (f32[384]{0:T(512)S(1)}, f32[384]{0:T(512)}, u32[]{:S(2)}) copy-start(f32[384]{0:T(512)} %gain_ref.1) | copy-start | bytes 4612
  57.1 13.7 %copy-start.6 = (f32[384]{0:T(512)S(1)}, f32[384]{0:T(512)}, u32[]{:S(2)}) copy-start(f32[384]{0:T(512)} %param.18) | copy-start | bytes 4612
  57.1 16.5 %copy-start = (bf16[32,384]{1,0:T(8,128)(2,1)S(1)}, bf16[32,384]{1,0:T(8,128)(2,1)}, u32[]{:S(2)}) copy-start(bf16[32,384]{1,0:T(8,128)(2,1)} %x_ref.1) | copy-start | bytes 73732
  59.9 13.8 %all-to-all-start.2 = ((bf16[16,32,384]{2,1,0:T(8,128)(2,1)}), bf16[16,32,384]{2,1,0:T(8,128)(2,1)S(1)}, u32[]{:S(2)}, u32[]{:S(2)}) async-start(bf16[16,32,384]{2,1,0:T(8,128)(2,1)} %bitcast.2), calls=%async_computation.2 | async-start | bytes 786432 | tf_op jit(solution)/shard_map/all_to_all | solution.py:376
  65.6 18.9 %collective-permute-start.2 = (bf16[1152,384]{1,0:T(8,128)(2,1)S(1)}, bf16[1152,384]{1,0:T(8,128)(2,1)S(1)}, u32[]{:S(2)}, u32[]{:S(2)}) collective-permute-start(bf16[1152,384]{1,0:T(8,128)(2,1)S(1)} %copy-done.7), channel_id=1, source_target_pairs={{0,0},{1,32},{32,1},{33,33},{2,2},{3,34},{34,3},{35,35},{4,4},{5,3... | collective-permute-start | bytes 2654216 | tf_op jit(solution)/shard_map/ppermute | solution.py:368
  74.5 11.6 %all-to-all-start.3 = ((bf16[16,32,384]{2,1,0:T(8,128)(2,1)}), bf16[16,32,384]{2,1,0:T(8,128)(2,1)S(1)}, u32[]{:S(2)}, u32[]{:S(2)}) async-start(bf16[16,32,384]{2,1,0:T(8,128)(2,1)} %get-tuple-element.18), calls=%async_computation.3 | async-start | bytes 786432 | tf_op jit(solution)/shard_map/all_to_all | solution.py:376
  84.4 6.0 %copy-start.2 = (bf16[1152,384]{1,0:T(8,128)(2,1)}, bf16[1152,384]{1,0:T(8,128)(2,1)S(1)}, u32[]{:S(2)}) copy-start(bf16[1152,384]{1,0:T(8,128)(2,1)S(1)} %collective-permute-done.2) | copy-start | bytes 2654212
  90.4 46.7 %all-to-all-start.4 = ((bf16[16,16,2432]{2,1,0:T(8,128)(2,1)}), bf16[16,16,2432]{2,1,0:T(8,128)(2,1)S(1)}, u32[]{:S(2)}, u32[]{:S(2)}) async-start(bf16[16,16,2432]{2,1,0:T(8,128)(2,1)} %bitcast.4), calls=%async_computation.4 | async-start | bytes 2490368 | tf_op jit(solution)/shard_map/all_to_all | solution.py:376
  98.6 45.5 %all-gather.11.cloned.1.call-start = ((), (), s32[]{:S(2)}) async-start(), calls=%async_computation.9 | async-start | bytes 2654208 | tf_op jit(solution)/shard_map/all_gather | solution.py:372
  138.9 23.8 %all-to-all-start.5 = ((bf16[16,16,1152]{2,1,0:T(8,128)(2,1)}), bf16[16,16,1152]{2,1,0:T(8,128)(2,1)S(1)}, u32[]{:S(2)}, u32[]{:S(2)}) async-start(bf16[16,16,1152]{2,1,0:T(8,128)(2,1)} %hidden.1), calls=%async_computation.5 | async-start | bytes 1179648 | tf_op jit(solution)/shard_map/all_to_all | solution.py:376
  162.6 17.1 %copy-start.5 = (f32[384]{0:T(512)S(1)}, f32[384]{0:T(512)}, u32[]{:S(2)}) copy-start(f32[384]{0:T(512)} %param.23) | copy-start | bytes 4612
Sparse Core Ops, SparseCore 0:
  28.3 21.2 all-gather.6
  57.2 20.0 all-gather.8
  101.5 20.1 all-gather.10

commit v3 on v2

v3 whole, which is shorter than its diff:
```python
import jax
import jax.numpy as jnp
from jax import lax
from jax.experimental import pallas as pl
from jax.experimental.pallas import tpu as pltpu
from jax.sharding import Mesh
from jax.sharding import PartitionSpec as P

D = 12288
GROUPS = 8
GROUP_HEADS = 12
HEAD_SIZE = 128
CONTEXT_SLOTS = 256
UNITS = 1152
WIDTH = 384
EXTRA = 128
PACK_SCALES = 768
PACK_ROWS = 784

ROWS = ("ylo", "x", "core")
COLS = ("b", "zl")
NEAR = ("ylo", "x")
SIDE = ("zl", "ylo", "x")
bf16 = jnp.bfloat16
f32 = jnp.float32

VMEM = pl.BlockSpec(memory_space=pltpu.VMEM)
SMEM = pl.BlockSpec(memory_space=pltpu.SMEM)
HBM = pl.BlockSpec(memory_space=pltpu.HBM)
PARAMS = pltpu.CompilerParams(vmem_limit_bytes=10 * 1024 * 1024)


def dot(a, b):
    return jnp.dot(a, b, preferred_element_type=f32)


def high_low(value):
    high = value.astype(bf16).astype(f32)
    return high, value - high


def in_hbm(array):
    return pltpu.with_memory_space_constraint(array, pltpu.HBM)


def attend_kernel(
    length_ref,
    query_in,
    latest_in,
    cache_ref,
    gate_up_ref,
    scale_ref,
    gain_ref,
    out_ref,
    packed_ref,
    query_row,
    latest_ref,
    query_ref,
    cache,
    unit_scale,
    gain,
    sems,
):
    small = [
        pltpu.make_async_copy(query_in, query_row, sems.at[2]),
        pltpu.make_async_copy(latest_in, latest_ref, sems.at[3]),
    ]
    copies = [
        pltpu.make_async_copy(cache_ref.at[0, part], cache.at[part], sems.at[part])
        for part in range(2)
    ]
    packs = [
        pltpu.make_async_copy(scale_ref, unit_scale, sems.at[4]),
        pltpu.make_async_copy(gain_ref, gain, sems.at[5]),
        pltpu.make_async_copy(gate_up_ref, packed_ref.at[pl.ds(0, PACK_SCALES), :], sems.at[6]),
    ]
    for copy in small + copies + packs:
        copy.start()
    for copy in small:
        copy.wait()
    for g in range(GROUPS):
        for h in range(GROUP_HEADS):
            at = (g * GROUP_HEADS + h) * HEAD_SIZE
            query_ref[g, h : h + 1] = query_row[:, at : at + HEAD_SIZE].astype(f32)
    scale = HEAD_SIZE ** (-0.5)
    slot = lax.broadcasted_iota(jnp.int32, (GROUP_HEADS, CONTEXT_SLOTS), 1)
    valid = slot < length_ref[0]
    lanes = [slice(g * HEAD_SIZE, (g + 1) * HEAD_SIZE) for g in range(GROUPS)]
    fresh = [
        jnp.sum(
            query_ref[g] * latest_ref[0, 0:1, lanes[g]].astype(f32),
            axis=1,
            keepdims=True,
        )
        * scale
        for g in range(GROUPS)
    ]
    copies[0].wait()
    cached = [
        jnp.where(
            valid,
            lax.dot_general(
                query_ref[g].astype(bf16),
                cache[0, :, lanes[g]],
                (((1,), (1,)), ((), ())),
                preferred_element_type=f32,
            )
            * scale,
            -jnp.inf,
        )
        for g in range(GROUPS)
    ]
    tops = [
        jnp.maximum(jnp.max(cached[g], axis=1, keepdims=True), fresh[g]) for g in range(GROUPS)
    ]
    weights = [jnp.exp(cached[g] - tops[g]) for g in range(GROUPS)]
    fresh = [jnp.exp(fresh[g] - tops[g]) for g in range(GROUPS)]
    inverse = [
        1.0 / (jnp.sum(weights[g], axis=1, keepdims=True) + fresh[g]) for g in range(GROUPS)
    ]
    probs = [(weights[g] * inverse[g]).astype(bf16) for g in range(GROUPS)]
    fresh = [(fresh[g] * inverse[g]).astype(bf16).astype(f32) for g in range(GROUPS)]
    copies[1].wait()
    mixed = [
        dot(probs[g], cache[1, :, lanes[g]])
        + fresh[g] * latest_ref[0, 1:2, lanes[g]].astype(f32)
        for g in range(GROUPS)
    ]
    for g in range(GROUPS):
        out_ref[g] = mixed[g].astype(bf16)


    packs[0].wait()
    packs[1].wait()
    rows = list(high_low(unit_scale[...]))
    for part in high_low(gain[...].reshape(1, WIDTH)):
        rows.append(jnp.concatenate([part, jnp.zeros((1, UNITS - WIDTH), f32)], axis=1))
    rows.append(jnp.zeros((10, UNITS), f32))
    packed_ref[PACK_SCALES:, :] = jnp.concatenate(rows, axis=0).astype(bf16)
    packs[2].wait()


def attend(
    query, latest_key_value, key_value_cache, lengths, gate_up_weight, gate_up_scale, ffn_gain
):
    return pl.pallas_call(
        attend_kernel,
        out_shape=(
            jax.ShapeDtypeStruct((GROUPS, GROUP_HEADS, HEAD_SIZE), bf16),
            pltpu.VMEM((PACK_ROWS, UNITS), bf16),
        ),
        in_specs=[SMEM] + [HBM] * 6,
        out_specs=(VMEM, VMEM),
        scratch_shapes=[
            pltpu.VMEM((1, D), bf16),
            pltpu.VMEM((1, 2, GROUPS * HEAD_SIZE), bf16),
            pltpu.VMEM((GROUPS, GROUP_HEADS, HEAD_SIZE), f32),
            pltpu.VMEM((2, CONTEXT_SLOTS, GROUPS * HEAD_SIZE), bf16),
            pltpu.VMEM((2, UNITS), f32),
            pltpu.VMEM((WIDTH,), f32),
            pltpu.SemaphoreType.DMA((7,)),
        ],
        compiler_params=PARAMS,
        name="attend",
    )(
        lengths,
        in_hbm(query),
        in_hbm(latest_key_value),
        in_hbm(key_value_cache),
        in_hbm(gate_up_weight),
        in_hbm(gate_up_scale),
        in_hbm(ffn_gain),
    )


def repeat_kernel(heads_ref, out_ref):
    half = GROUP_HEADS // 2
    for z in range(2):
        for j in range(half):
            block = heads_ref[:, z * half + j, :]
            for b in range(16):
                out_ref[2 * b + z, :, j * HEAD_SIZE : (j + 1) * HEAD_SIZE] = block


def repeat(heads):
    return pl.pallas_call(
        repeat_kernel,
        out_shape=jax.ShapeDtypeStruct((32, 8, 768), bf16),
        in_specs=[VMEM],
        out_specs=VMEM,
        compiler_params=PARAMS,
        name="repeat",
    )(heads)


def project_kernel(attn_ref, own_ref, other_ref, out_ref):
    row = lax.broadcasted_iota(jnp.int32, (256, 256), 0)
    source = (row & 31) * 8 + (row >> 5)
    pick = (lax.broadcasted_iota(jnp.int32, (256, 256), 1) == source).astype(f32).astype(bf16)
    attn = attn_ref[...].astype(f32).reshape(256, 768).astype(bf16)
    attn = dot(pick, attn).astype(bf16)
    core = lax.axis_index("core")
    out_ref[core] = dot(attn, own_ref[...]).astype(bf16)
    out_ref[1 - core] = dot(attn, other_ref[...]).astype(bf16)


def project(attn, own, other):
    return pl.pallas_call(
        project_kernel,
        out_shape=jax.ShapeDtypeStruct((2, 256, WIDTH), bf16),
        in_specs=[VMEM, VMEM, VMEM],
        out_specs=VMEM,
        compiler_params=PARAMS,
        name="project",
    )(attn, own, other)


def stream_kernel(parts_ref, x_ref, scale_ref, gain_ref, stream_ref, out_ref):
    attended = parts_ref[0].astype(f32)
    for s in range(1, 16):
        attended = attended + parts_ref[s].astype(f32)
    stream = x_ref[...].astype(f32) + attended * scale_ref[...]
    stream_ref[...] = stream
    gained = (stream * gain_ref[...]).astype(bf16)
    for s in range(16):
        out_ref[s] = gained


def stream_and_spread(parts, x_in, o_scale, ffn_gain):
    return pl.pallas_call(
        stream_kernel,
        out_shape=(
            jax.ShapeDtypeStruct((32, WIDTH), f32),
            jax.ShapeDtypeStruct((16, 32, WIDTH), bf16),
        ),
        in_specs=[VMEM] * 4,
        out_specs=(VMEM, VMEM),
        compiler_params=PARAMS,
        name="stream",
    )(parts, x_in, o_scale[None], ffn_gain[None])


def stage(after, *arrays):
    count = len(arrays)

    def kernel(after_ref, *refs):
        sems = refs[-1]
        copies = [
            pltpu.make_async_copy(refs[n], refs[count + n], sems.at[n]) for n in range(count)
        ]
        for copy in copies:
            copy.start()
        for copy in copies:
            copy.wait()

    return pl.pallas_call(
        kernel,
        out_shape=[pltpu.VMEM(array.shape, array.dtype) for array in arrays],
        in_specs=[pl.BlockSpec(memory_space=pl.ANY)] + [HBM] * count,
        out_specs=[VMEM] * count,
        scratch_shapes=[pltpu.SemaphoreType.DMA((count,))],
        compiler_params=PARAMS,
        name="stage",
    )(after, *[in_hbm(array) for array in arrays])


def gate_up_kernel(rows_ref, own_ref, other_ref, out_ref):
    core = lax.axis_index("core")
    weights = (own_ref, other_ref)
    rows = [
        rows_ref[pl.ds(at * 8, 8)].reshape(256, WIDTH) for at in (core, 1 - core)
    ]
    both_rows = jnp.concatenate(rows, axis=1)
    for k in range(2):
        for at, size in ((0, 512), (512, 640)):
            weight = jnp.concatenate(
                [ref[k * WIDTH : (k + 1) * WIDTH, at : at + size] for ref in weights], axis=0
            )
            out_ref[:, k * UNITS + at : k * UNITS + at + size] = dot(both_rows, weight).astype(
                bf16
            )
    squares = jnp.zeros((256, 1), f32)
    for half in range(2):
        gain = weights[half][PACK_SCALES:, :WIDTH].astype(f32)
        gain = gain[4:5] + gain[5:6]
        scaled = rows[half].astype(f32) * (1.0 / gain)
        squares = squares + jnp.sum(scaled * scaled, axis=1, keepdims=True)
    high, low = high_low(squares)
    lane = lax.broadcasted_iota(jnp.int32, (256, EXTRA), 1)
    out_ref[:, 2 * UNITS :] = jnp.where(
        lane == 0, high, jnp.where(lane == 1, low, 0.0)
    ).astype(bf16)


def gate_up(rows, own, other):
    return pl.pallas_call(
        gate_up_kernel,
        out_shape=jax.ShapeDtypeStruct((256, 2 * UNITS + EXTRA), bf16),
        in_specs=[VMEM] * 3,
        out_specs=VMEM,
        compiler_params=PARAMS,
        name="gate_up",
    )(rows, own, other)


def hidden_kernel(shares_ref, scales_ref, out_ref):
    extra = shares_ref[0, :, 2 * UNITS :].astype(f32)
    for s in range(1, 16):
        extra = extra + shares_ref[s, :, 2 * UNITS :].astype(f32)
    squares = jnp.sum(extra, axis=1, keepdims=True)
    inverse = lax.rsqrt(squares / D + 1e-05)
    scales = scales_ref[...].astype(f32)
    scales = scales[0:2] + scales[2:4]
    for j in range(3):
        parts = []
        for k in range(2):
            lanes = slice((k * 3 + j) * WIDTH, (k * 3 + j + 1) * WIDTH)
            total = shares_ref[0, :, lanes].astype(f32)
            for s in range(1, 16):
                total = total + shares_ref[s, :, lanes].astype(f32)
            parts.append(total * inverse * scales[k : k + 1, j * WIDTH : (j + 1) * WIDTH])
        gate, up = parts
        hidden = (gate / (1.0 + jnp.exp(-gate)) * up).astype(bf16)
        for b in range(16):
            out_ref[b, :, j * WIDTH : (j + 1) * WIDTH] = hidden


def hidden_and_spread(shares, scales):
    return pl.pallas_call(
        hidden_kernel,
        out_shape=jax.ShapeDtypeStruct((16, 16, UNITS), bf16),
        in_specs=[VMEM, VMEM],
        out_specs=VMEM,
        compiler_params=PARAMS,
        name="hidden",
    )(shares, scales)


def down_kernel(hidden_ref, own_ref, other_ref, out_ref):
    core = lax.axis_index("core")
    hidden = hidden_ref[...].reshape(256, UNITS)
    out_ref[core] = dot(hidden, own_ref[...]).astype(bf16)
    out_ref[1 - core] = dot(hidden, other_ref[...]).astype(bf16)


def down(hidden, own, other):
    return pl.pallas_call(
        down_kernel,
        out_shape=jax.ShapeDtypeStruct((2, 256, WIDTH), bf16),
        in_specs=[VMEM, VMEM, VMEM],
        out_specs=VMEM,
        compiler_params=PARAMS,
        name="down",
    )(hidden, own, other)


def swap(block):
    return lax.ppermute(block, ("core", "zl"), [(0, 0), (1, 2), (2, 1), (3, 3)])


def other_core(block):
    return lax.ppermute(block, "core", [(0, 1), (1, 0)])


def exchange(parts, axis):
    return lax.all_to_all(parts, axis, split_axis=0, concat_axis=0, tiled=False)


def body(
    x_in,
    query,
    latest_key_value,
    key_value_cache,
    lengths,
    o_weight,
    o_scale,
    ffn_gain,
    gate_up_weight,
    gate_up_scale,
    down_weight,
    down_scale,
):
    own_o = swap(o_weight)
    heads, packed = attend(
        query,
        latest_key_value,
        key_value_cache,
        lengths,
        gate_up_weight.reshape(2 * WIDTH, UNITS),
        gate_up_scale,
        ffn_gain,
    )
    heads, own_o, packed = lax.optimization_barrier((heads, own_o, packed))
    other_o = other_core(own_o)
    own_gate_up = swap(packed)
    heads = exchange(heads, NEAR)
    attn = exchange(repeat(heads), COLS)
    attn, down_weight = lax.optimization_barrier((attn, down_weight))
    own_down = swap(down_weight)
    parts = project(attn, own_o, other_o)
    other_gate_up = other_core(own_gate_up)
    parts = exchange(parts.reshape(16, 32, WIDTH), SIDE)
    stream, rows = stream_and_spread(parts, x_in, o_scale, ffn_gain)
    (other_gate_up,) = stage(stream, other_gate_up)
    rows = exchange(rows, SIDE)
    rows, own_down = lax.optimization_barrier((rows, own_down))
    other_down = other_core(own_down)
    shares = exchange(
        gate_up(rows, own_gate_up, other_gate_up).reshape(16, 16, 2 * UNITS + EXTRA), "b"
    )
    hidden = hidden_and_spread(shares, own_gate_up[PACK_SCALES:])
    own_down, other_down = stage(hidden, own_down, other_down)
    hidden = exchange(hidden, "b")
    parts = exchange(down(hidden, own_down, other_down).reshape(16, 32, WIDTH), SIDE)
    lowered = jnp.sum(parts.astype(f32), axis=0)
    return (stream + lowered * down_scale).astype(bf16)


def solution(mesh):
    mesh = Mesh(mesh.devices.reshape(2, 4, 2, 16, 2), ("ylo", "x", "core", "b", "zl"))
    everywhere = ROWS + COLS
    in_specs = (
        P(ROWS, COLS),
        P(everywhere, None),
        P(everywhere, None, None),
        P(everywhere, None, None, None),
        P(everywhere),
        P(ROWS, COLS),
        P(COLS),
        P(COLS),
        P(None, COLS, ROWS),
        P(None, ROWS),
        P(ROWS, COLS),
        P(COLS),
    )
    out_specs = P(ROWS, COLS)
    return jax.shard_map(body, mesh=mesh, in_specs=in_specs, out_specs=out_specs, check_vma=False)
```

time: 188 us -> 182 us (0.968)
  blocking collectives: 52.3 us -> 22.8 us
  starting transfers between devices: 35.2 us -> 59.9 us
  between operations: 14 us -> 0.83 us
  waiting for transfers between devices: 67.9 us -> 80.9 us
    all_to_all x3 -> x2, blocking collectives: 52.3 us -> 22.8 us  [exchange(): return lax.all_to_all(parts, axis, split_axis=0, concat_axis=0, tiled=False)]
    all_to_all x4 -> x5, starting transfers between devices: 22.6 us -> 37.9 us  [exchange(): return lax.all_to_all(parts, axis, split_axis=0, concat_axis=0, tiled=False)]
    all_to_all x4 -> x5, waiting for transfers between devices: 60.8 us -> 72.8 us  [exchange(): return lax.all_to_all(parts, axis, split_axis=0, concat_axis=0, tiled=False)]
    ppermute x0 -> x3, starting transfers between devices: none -> 7.46 us  [other_core(): return lax.ppermute(block, 'core', [(0, 1), (1, 0)])]
    pallas_call x2 -> x3, Pallas kernels: 2.86 us -> 6.13 us  [the longest x1 3.18 us: attend(): pl.pallas_call(attend_kernel, out_shape=(jax.ShapeDtypeStruct((GROUPS, GR...]
    ppermute x0 -> x3, waiting for transfers between devices: none -> 2.25 us  [other_core(): return lax.ppermute(block, 'core', [(0, 1), (1, 0)])]
    pallas_call x1, Pallas kernels: 4.3 us -> 2.28 us  [gate_up(): pl.pallas_call(gate_up_kernel, out_shape=jax.ShapeDtypeStruct((256, 2 * U...]
    ppermute x3, starting transfers between devices: 12.6 us -> 14.6 us  [swap(): return lax.ppermute(block, ('core', 'zl'), [(0, 0), (1, 2), (2, 1), (3, 3)])]
  transfers between devices with their start and end apart: 10 -> 11, of which waited for: 5 -> 8; matrix products, arithmetic and copies ran while one was open for 0% -> 0% of each run, Pallas kernels for 4% -> 5%
where the time goes in v3:
time: 182 us; the launch traced here: 181 us
  waiting for transfers between devices  80.9 us (44%)
  starting transfers between devices  59.9 us (33%)
  blocking collectives  22.8 us (13%)
  Pallas kernels  14.5 us (8%)
    all_to_all x5, waiting for transfers between devices, exchange(): return lax.all_to_all(parts, axis, split_axis=0, concat_axis=0, tiled=False)  72.8 us
    all_to_all x5, starting transfers between devices, exchange(): return lax.all_to_all(parts, axis, split_axis=0, concat_axis=0, tiled=False)  37.9 us
    all_to_all x2, blocking collectives, exchange(): return lax.all_to_all(parts, axis, split_axis=0, concat_axis=0, tiled=False)  22.8 us
    ppermute x3, starting transfers between devices, swap(): return lax.ppermute(block, ('core', 'zl'), [(0, 0), (1, 2), (2, 1), (3, 3)])  14.6 us
    ppermute x3, starting transfers between devices, other_core(): return lax.ppermute(block, 'core', [(0, 1), (1, 0)])  7.46 us
    ppermute x3, waiting for transfers between devices, swap(): return lax.ppermute(block, ('core', 'zl'), [(0, 0), (1, 2), (2, 1), (3, 3)])  5.87 us
  transfers between devices with their start and end apart: 11, of which 8 were waited for; matrix products, arithmetic and copies ran while one was open for 0% of the time, Pallas kernels for 5%

profile of v3, /device:TPU:1, one launch (start us, length us, event | category | flops | bytes accessed | tf_op | source)
XLA Modules:
  0.0 180.6 jit_solution(2868567331860379028)
XLA Ops:
  0.0 5.4 %collective-permute-start = (bf16[768,384]{1,0:T(8,128)(2,1)}, bf16[768,384]{1,0:T(8,128)(2,1)S(1)}, u32[]{:S(2)}, u32[]{:S(2)}) collective-permute-start(bf16[768,384]{1,0:T(8,128)(2,1)} %param.17), channel_id=1, source_target_pairs={{0,0},{1,32},{32,1},{33,33},{2,2},{3,34},{34,3},{35,35},{4,4},{5,3... | collective-permute-start | bytes 1769480 | tf_op jit(solution)/shard_map/ppermute | solution.py:358
  6.0 3.2 %attend.1 = (bf16[8,12,128]{2,1,0:T(8,128)(2,1)S(1)}, bf16[784,1152]{1,0:T(8,128)(2,1)}) custom-call(s32[1]{0:T(128)S(6)} %copy.13.length_ref, bf16[1,12288]{1,0:T(2,128)(2,1)} %query_in.1, bf16[1,2,1024]{2,1,0:T(2,128)(2,1)} %latest_in.1, bf16[1,2,256,1024]{3,2,1,0:T(8,128)(2,1)} %cache_ref.1, bf16[768,1152]{1,0:T(8,128)(2,1)} %bitcast.5, ...), custom_call_target="tpu_custom_call" | custom-call | tf_op jit(solution)/shard_map/attend/pallas_call | solution.py:146
  9.2 3.9 %collective-permute-done.own_ref = bf16[768,384]{1,0:T(8,128)(2,1)S(1)} collective-permute-done((bf16[768,384]{1,0:T(8,128)(2,1)}, bf16[768,384]{1,0:T(8,128)(2,1)S(1)}, u32[]{:S(2)}, u32[]{:S(2)}) %collective-permute-start) | collective-permute-done | bytes 589856 | tf_op jit(solution)/shard_map/ppermute | solution.py:358
  13.1 3.6 %collective-permute-start.3 = (bf16[784,1152]{1,0:T(8,128)(2,1)}, bf16[784,1152]{1,0:T(8,128)(2,1)S(1)}, u32[]{:S(2)}, u32[]{:S(2)}) collective-permute-start(bf16[784,1152]{1,0:T(8,128)(2,1)} %get-tuple-element.27), channel_id=1, source_target_pairs={{0,0},{1,32},{32,1},{33,33},{2,2},{3,34},{34,3},{35,35},{4,4},{5,3... | collective-permute-start | bytes 5419016 | tf_op jit(solution)/shard_map/ppermute | solution.py:358
  16.8 9.9 %all_to_all.35.heads_ref = bf16[8,12,128]{2,1,0:T(8,128)(2,1)S(1)} all-to-all(bf16[8,12,128]{2,1,0:T(8,128)(2,1)S(1)} %get-tuple-element.20), channel_id=1, replica_groups=mesh['ylo'=2,'x'=4,'core'=2,'b'=16,'zl'=2] {'ylo','x'}, dimensions={0} | all-to-all | bytes 49152 | tf_op jit(solution)/shard_map/all_to_all | solution.py:366
  26.7 0.8 repeat.1
  27.6 14.0 %all-to-all-start.1 = ((bf16[32,8,768]{2,1,0:T(8,128)(2,1)}), bf16[32,8,768]{2,1,0:T(8,128)(2,1)S(1)}, u32[]{:S(2)}, u32[]{:S(2)}) async-start(bf16[32,8,768]{2,1,0:T(8,128)(2,1)} %repeat.1), calls=%async_computation.1 | async-start | bytes 786432 | tf_op jit(solution)/shard_map/all_to_all | solution.py:366
  41.6 2.6 %collective-permute-start.1 = (bf16[768,384]{1,0:T(8,128)(2,1)S(1)}, bf16[768,384]{1,0:T(8,128)(2,1)}, u32[]{:S(2)}, u32[]{:S(2)}) collective-permute-start(bf16[768,384]{1,0:T(8,128)(2,1)S(1)} %collective-permute-done.own_ref), channel_id=1, source_target_pairs={{0,32},{32,0},{1,33},{33,1},{2,34},{34,2},{3,35},{35,3},{4,36},{36... | collective-permute-start | bytes 1769480 | tf_op jit(solution)/shard_map/ppermute | solution.py:362
  44.2 1.9 %collective-permute-start.4 = (bf16[784,1152]{1,0:T(8,128)(2,1)S(1)}, bf16[784,1152]{1,0:T(8,128)(2,1)}, u32[]{:S(2)}, u32[]{:S(2)}) collective-permute-start(bf16[784,1152]{1,0:T(8,128)(2,1)S(1)} %collective-permute-done.3.own_ref), channel_id=1, source_target_pairs={{0,32},{32,0},{1,33},{33,1},{2,34},{34,2},{3,35},{35,3},{4,36},{36... | collective-permute-start | bytes 5419016 | tf_op jit(solution)/shard_map/ppermute | solution.py:362
  46.1 10.4 %all-to-all-done.1.attn_ref = bf16[32,8,768]{2,1,0:T(8,128)(2,1)S(1)} async-done(((bf16[32,8,768]{2,1,0:T(8,128)(2,1)}), bf16[32,8,768]{2,1,0:T(8,128)(2,1)S(1)}, u32[]{:S(2)}, u32[]{:S(2)}) %all-to-all-start.1) | async-done | bytes 393248 | tf_op jit(solution)/shard_map/all_to_all | solution.py:366
  56.5 2.5 %project.1 = bf16[2,256,384]{2,1,0:T(8,128)(2,1)} custom-call(bf16[32,8,768]{2,1,0:T(8,128)(2,1)S(1)} %all-to-all-done.1.attn_ref, bf16[768,384]{1,0:T(8,128)(2,1)S(1)} %collective-permute-done.own_ref, bf16[768,384]{1,0:T(8,128)(2,1)} %collective-permute-done.1.other_ref), custom_call_target="tpu_custom_call" | custom-call | tf_op jit(solution)/shard_map/project/pallas_call | solution.py:208
  59.0 4.2 %all-to-all-start.2 = ((bf16[16,32,384]{2,1,0:T(8,128)(2,1)}), bf16[16,32,384]{2,1,0:T(8,128)(2,1)S(1)}, u32[]{:S(2)}, u32[]{:S(2)}) async-start(bf16[16,32,384]{2,1,0:T(8,128)(2,1)} %bitcast.1), calls=%async_computation.2 | async-start | bytes 786432 | tf_op jit(solution)/shard_map/all_to_all | solution.py:366
  63.2 5.6 %collective-permute-start.2 = (bf16[1152,384]{1,0:T(8,128)(2,1)}, bf16[1152,384]{1,0:T(8,128)(2,1)}, u32[]{:S(2)}, u32[]{:S(2)}) collective-permute-start(bf16[1152,384]{1,0:T(8,128)(2,1)} %param.22), channel_id=1, source_target_pairs={{0,0},{1,32},{32,1},{33,33},{2,2},{3,34},{34,3},{35,35},{4,4},{5,3... | collective-permute-start | bytes 2654216 | tf_op jit(solution)/shard_map/ppermute | solution.py:358
  68.8 2.8 %all-to-all-done.2.parts_ref = bf16[16,32,384]{2,1,0:T(8,128)(2,1)S(1)} async-done(((bf16[16,32,384]{2,1,0:T(8,128)(2,1)}), bf16[16,32,384]{2,1,0:T(8,128)(2,1)S(1)}, u32[]{:S(2)}, u32[]{:S(2)}) %all-to-all-start.2) | async-done | bytes 393248 | tf_op jit(solution)/shard_map/all_to_all | solution.py:366
  71.6 0.8 stream.1
  72.4 5.9 %all-to-all-start.3 = ((bf16[16,32,384]{2,1,0:T(8,128)(2,1)}), bf16[16,32,384]{2,1,0:T(8,128)(2,1)S(1)}, u32[]{:S(2)}, u32[]{:S(2)}) async-start(bf16[16,32,384]{2,1,0:T(8,128)(2,1)} %get-tuple-element.24), calls=%async_computation.3 | async-start | bytes 786432 | tf_op jit(solution)/shard_map/all_to_all | solution.py:366
  78.4 1.9 %collective-permute-done.2.refs_0_ = bf16[1152,384]{1,0:T(8,128)(2,1)} collective-permute-done((bf16[1152,384]{1,0:T(8,128)(2,1)}, bf16[1152,384]{1,0:T(8,128)(2,1)}, u32[]{:S(2)}, u32[]{:S(2)}) %collective-permute-start.2) | collective-permute-done | bytes 884768 | tf_op jit(solution)/shard_map/ppermute | solution.py:358
  80.3 6.2 %all-to-all-done.3.rows_ref = bf16[16,32,384]{2,1,0:T(8,128)(2,1)S(1)} async-done(((bf16[16,32,384]{2,1,0:T(8,128)(2,1)}), bf16[16,32,384]{2,1,0:T(8,128)(2,1)S(1)}, u32[]{:S(2)}, u32[]{:S(2)}) %all-to-all-start.3) | async-done | bytes 393248 | tf_op jit(solution)/shard_map/all_to_all | solution.py:366
  86.5 1.5 stage.2.other_ref
  88.0 2.3 %gate_up.1 = bf16[256,2432]{1,0:T(8,128)(2,1)} custom-call(bf16[16,32,384]{2,1,0:T(8,128)(2,1)S(1)} %all-to-all-done.3.rows_ref, bf16[784,1152]{1,0:T(8,128)(2,1)S(1)} %collective-permute-done.3.own_ref, bf16[784,1152]{1,0:T(8,128)(2,1)S(1)} %stage.2.other_ref), custom_call_target="tpu_custom_call" | custom-call | tf_op jit(solution)/shard_map/gate_up/pallas_call | solution.py:296
  90.3 8.1 %all-to-all-start.4 = ((bf16[16,16,2432]{2,1,0:T(8,128)(2,1)}), bf16[16,16,2432]{2,1,0:T(8,128)(2,1)S(1)}, u32[]{:S(2)}, u32[]{:S(2)}) async-start(bf16[16,16,2432]{2,1,0:T(8,128)(2,1)} %bitcast.2), calls=%async_computation.4 | async-start | bytes 2490368 | tf_op jit(solution)/shard_map/all_to_all | solution.py:366
  98.4 38.4 %all-to-all-done.4.shares_ref = bf16[16,16,2432]{2,1,0:T(8,128)(2,1)S(1)} async-done(((bf16[16,16,2432]{2,1,0:T(8,128)(2,1)}), bf16[16,16,2432]{2,1,0:T(8,128)(2,1)S(1)}, u32[]{:S(2)}, u32[]{:S(2)}) %all-to-all-start.4) | async-done | bytes 1245216 | tf_op jit(solution)/shard_map/all_to_all | solution.py:366
  136.8 1.1 hidden.1.after_ref
  137.9 5.7 %all-to-all-start.5 = ((bf16[16,16,1152]{2,1,0:T(8,128)(2,1)}), bf16[16,16,1152]{2,1,0:T(8,128)(2,1)S(1)}, u32[]{:S(2)}, u32[]{:S(2)}) async-start(bf16[16,16,1152]{2,1,0:T(8,128)(2,1)} %hidden.1.after_ref), calls=%async_computation.5 | async-start | bytes 1179648 | tf_op jit(solution)/shard_map/all_to_all | solution.py:366
  143.6 3.0 %collective-permute-start.5 = (bf16[1152,384]{1,0:T(8,128)(2,1)}, bf16[1152,384]{1,0:T(8,128)(2,1)S(1)}, u32[]{:S(2)}, u32[]{:S(2)}) collective-permute-start(bf16[1152,384]{1,0:T(8,128)(2,1)} %collective-permute-done.2.refs_0_), channel_id=1, source_target_pairs={{0,32},{32,0},{1,33},{33,1},{2,34},{34,2},{3,35},{35,3},{4,36},{36... | collective-permute-start | bytes 2654216 | tf_op jit(solution)/shard_map/ppermute | solution.py:362
  146.5 2.2 %collective-permute-done.5.refs_1_ = bf16[1152,384]{1,0:T(8,128)(2,1)S(1)} collective-permute-done((bf16[1152,384]{1,0:T(8,128)(2,1)}, bf16[1152,384]{1,0:T(8,128)(2,1)S(1)}, u32[]{:S(2)}, u32[]{:S(2)}) %collective-permute-start.5) | collective-permute-done | bytes 884768 | tf_op jit(solution)/shard_map/ppermute | solution.py:362
  148.8 0.9 copy-done.1
  149.7 1.4 stage.3
  151.2 15.0 %all-to-all-done.5.hidden_ref = bf16[16,16,1152]{2,1,0:T(8,128)(2,1)S(1)} async-done(((bf16[16,16,1152]{2,1,0:T(8,128)(2,1)}), bf16[16,16,1152]{2,1,0:T(8,128)(2,1)S(1)}, u32[]{:S(2)}, u32[]{:S(2)}) %all-to-all-start.5) | async-done | bytes 589856 | tf_op jit(solution)/shard_map/all_to_all | solution.py:366
  166.2 0.8 down.1
  167.0 12.9 %all_to_all.36 = bf16[16,32,384]{2,1,0:T(8,128)(2,1)S(1)} all-to-all(bf16[16,32,384]{2,1,0:T(8,128)(2,1)S(1)} %bitcast.4), channel_id=1, replica_groups=mesh['ylo'=2,'x'=4,'core'=2,'b'=16,'zl'=2] {'zl','ylo','x'}, dimensions={0} | all-to-all | bytes 786432 | tf_op jit(solution)/shard_map/all_to_all | solution.py:366
  180.0 0.6 add_convert_fusion
  (16 shorter events, 0.1 us)
Async XLA Ops:
  0.0 13.1 %collective-permute-start = (bf16[768,384]{1,0:T(8,128)(2,1)}, bf16[768,384]{1,0:T(8,128)(2,1)S(1)}, u32[]{:S(2)}, u32[]{:S(2)}) collective-permute-start(bf16[768,384]{1,0:T(8,128)(2,1)} %param.17), channel_id=1, source_target_pairs={{0,0},{1,32},{32,1},{33,33},{2,2},{3,34},{34,3},{35,35},{4,4},{5,3... | collective-permute-start | bytes 1769480 | tf_op jit(solution)/shard_map/ppermute | solution.py:358
  13.1 31.0 %collective-permute-start.3 = (bf16[784,1152]{1,0:T(8,128)(2,1)}, bf16[784,1152]{1,0:T(8,128)(2,1)S(1)}, u32[]{:S(2)}, u32[]{:S(2)}) collective-permute-start(bf16[784,1152]{1,0:T(8,128)(2,1)} %get-tuple-element.27), channel_id=1, source_target_pairs={{0,0},{1,32},{32,1},{33,33},{2,2},{3,34},{34,3},{35,35},{4,4},{5,3... | collective-permute-start | bytes 5419016 | tf_op jit(solution)/shard_map/ppermute | solution.py:358
  27.6 41.2 %copy-start.2 = (f32[384]{0:T(512)S(1)}, f32[384]{0:T(512)}, u32[]{:S(2)}) copy-start(f32[384]{0:T(512)} %gain_ref.1) | copy-start | bytes 4612
  27.6 41.2 %copy-start.4 = (f32[384]{0:T(512)S(1)}, f32[384]{0:T(512)}, u32[]{:S(2)}) copy-start(f32[384]{0:T(512)} %param.18) | copy-start | bytes 4612
  27.6 44.1 %copy-start = (bf16[32,384]{1,0:T(8,128)(2,1)S(1)}, bf16[32,384]{1,0:T(8,128)(2,1)}, u32[]{:S(2)}) copy-start(bf16[32,384]{1,0:T(8,128)(2,1)} %x_ref.1) | copy-start | bytes 73732
  27.6 28.9 %all-to-all-start.1 = ((bf16[32,8,768]{2,1,0:T(8,128)(2,1)}), bf16[32,8,768]{2,1,0:T(8,128)(2,1)S(1)}, u32[]{:S(2)}, u32[]{:S(2)}) async-start(bf16[32,8,768]{2,1,0:T(8,128)(2,1)} %repeat.1), calls=%async_computation.1 | async-start | bytes 786432 | tf_op jit(solution)/shard_map/all_to_all | solution.py:366
  41.6 14.9 %collective-permute-start.1 = (bf16[768,384]{1,0:T(8,128)(2,1)S(1)}, bf16[768,384]{1,0:T(8,128)(2,1)}, u32[]{:S(2)}, u32[]{:S(2)}) collective-permute-start(bf16[768,384]{1,0:T(8,128)(2,1)S(1)} %collective-permute-done.own_ref), channel_id=1, source_target_pairs={{0,32},{32,0},{1,33},{33,1},{2,34},{34,2},{3,35},{35,3},{4,36},{36... | collective-permute-start | bytes 1769480 | tf_op jit(solution)/shard_map/ppermute | solution.py:362
  44.2 42.3 %collective-permute-start.4 = (bf16[784,1152]{1,0:T(8,128)(2,1)S(1)}, bf16[784,1152]{1,0:T(8,128)(2,1)}, u32[]{:S(2)}, u32[]{:S(2)}) collective-permute-start(bf16[784,1152]{1,0:T(8,128)(2,1)S(1)} %collective-permute-done.3.own_ref), channel_id=1, source_target_pairs={{0,32},{32,0},{1,33},{33,1},{2,34},{34,2},{3,35},{35,3},{4,36},{36... | collective-permute-start | bytes 5419016 | tf_op jit(solution)/shard_map/ppermute | solution.py:362
  59.0 12.6 %all-to-all-start.2 = ((bf16[16,32,384]{2,1,0:T(8,128)(2,1)}), bf16[16,32,384]{2,1,0:T(8,128)(2,1)S(1)}, u32[]{:S(2)}, u32[]{:S(2)}) async-start(bf16[16,32,384]{2,1,0:T(8,128)(2,1)} %bitcast.1), calls=%async_computation.2 | async-start | bytes 786432 | tf_op jit(solution)/shard_map/all_to_all | solution.py:366
  63.2 17.1 %collective-permute-start.2 = (bf16[1152,384]{1,0:T(8,128)(2,1)}, bf16[1152,384]{1,0:T(8,128)(2,1)}, u32[]{:S(2)}, u32[]{:S(2)}) collective-permute-start(bf16[1152,384]{1,0:T(8,128)(2,1)} %param.22), channel_id=1, source_target_pairs={{0,0},{1,32},{32,1},{33,33},{2,2},{3,34},{34,3},{35,35},{4,4},{5,3... | collective-permute-start | bytes 2654216 | tf_op jit(solution)/shard_map/ppermute | solution.py:358
  72.4 14.0 %all-to-all-start.3 = ((bf16[16,32,384]{2,1,0:T(8,128)(2,1)}), bf16[16,32,384]{2,1,0:T(8,128)(2,1)S(1)}, u32[]{:S(2)}, u32[]{:S(2)}) async-start(bf16[16,32,384]{2,1,0:T(8,128)(2,1)} %get-tuple-element.24), calls=%async_computation.3 | async-start | bytes 786432 | tf_op jit(solution)/shard_map/all_to_all | solution.py:366
  90.3 46.5 %all-to-all-start.4 = ((bf16[16,16,2432]{2,1,0:T(8,128)(2,1)}), bf16[16,16,2432]{2,1,0:T(8,128)(2,1)S(1)}, u32[]{:S(2)}, u32[]{:S(2)}) async-start(bf16[16,16,2432]{2,1,0:T(8,128)(2,1)} %bitcast.2), calls=%async_computation.4 | async-start | bytes 2490368 | tf_op jit(solution)/shard_map/all_to_all | solution.py:366
  137.9 28.3 %all-to-all-start.5 = ((bf16[16,16,1152]{2,1,0:T(8,128)(2,1)}), bf16[16,16,1152]{2,1,0:T(8,128)(2,1)S(1)}, u32[]{:S(2)}, u32[]{:S(2)}) async-start(bf16[16,16,1152]{2,1,0:T(8,128)(2,1)} %hidden.1.after_ref), calls=%async_computation.5 | async-start | bytes 1179648 | tf_op jit(solution)/shard_map/all_to_all | solution.py:366
  143.6 5.2 %collective-permute-start.5 = (bf16[1152,384]{1,0:T(8,128)(2,1)}, bf16[1152,384]{1,0:T(8,128)(2,1)S(1)}, u32[]{:S(2)}, u32[]{:S(2)}) collective-permute-start(bf16[1152,384]{1,0:T(8,128)(2,1)} %collective-permute-done.2.refs_0_), channel_id=1, source_target_pairs={{0,32},{32,0},{1,33},{33,1},{2,34},{34,2},{3,35},{35,3},{4,36},{36... | collective-permute-start | bytes 2654216 | tf_op jit(solution)/shard_map/ppermute | solution.py:362
  148.8 0.9 copy-start.1
  166.2 13.8 %copy-start.3 = (f32[384]{0:T(512)S(1)}, f32[384]{0:T(512)}, u32[]{:S(2)}) copy-start(f32[384]{0:T(512)} %param.23) | copy-start | bytes 4612

commit v4 on v3

--- a/solution.py
+++ b/solution.py
@@ -193,7 +193,9 @@
     )(heads)
 
 
-def project_kernel(attn_ref, own_ref, other_ref, out_ref):
+def project_kernel(attn_ref, own_ref, other_in, out_ref, other_ref, sem):
+    load = pltpu.make_async_copy(other_in, other_ref, sem.at[0])
+    load.start()
     row = lax.broadcasted_iota(jnp.int32, (256, 256), 0)
     source = (row & 31) * 8 + (row >> 5)
     pick = (lax.broadcasted_iota(jnp.int32, (256, 256), 1) == source).astype(f32).astype(bf16)
@@ -201,6 +203,7 @@
     attn = dot(pick, attn).astype(bf16)
     core = lax.axis_index("core")
     out_ref[core] = dot(attn, own_ref[...]).astype(bf16)
+    load.wait()
     out_ref[1 - core] = dot(attn, other_ref[...]).astype(bf16)
 
 
@@ -208,11 +211,12 @@
     return pl.pallas_call(
         project_kernel,
         out_shape=jax.ShapeDtypeStruct((2, 256, WIDTH), bf16),
-        in_specs=[VMEM, VMEM, VMEM],
+        in_specs=[VMEM, VMEM, HBM],
         out_specs=VMEM,
+        scratch_shapes=[pltpu.VMEM((768, WIDTH), bf16), pltpu.SemaphoreType.DMA((1,))],
         compiler_params=PARAMS,
         name="project",
-    )(attn, own, other)
+    )(attn, own, in_hbm(other))
 
 
 def stream_kernel(parts_ref, x_ref, scale_ref, gain_ref, stream_ref, out_ref):
@@ -264,21 +268,35 @@
     )(after, *[in_hbm(array) for array in arrays])
 
 
-def gate_up_kernel(rows_ref, own_ref, other_ref, out_ref):
+def gate_up_kernel(rows_ref, own_ref, other_in, out_ref, other_ref, total, sems):
+    cuts = ((PACK_SCALES, 16), (0, WIDTH), (WIDTH, WIDTH))
+    loads = [
+        pltpu.make_async_copy(
+            other_in.at[pl.ds(at, size), :], other_ref.at[pl.ds(at, size), :], sems.at[n]
+        )
+        for n, (at, size) in enumerate(cuts)
+    ]
+    for load in loads:
+        load.start()
     core = lax.axis_index("core")
     weights = (own_ref, other_ref)
     rows = [
         rows_ref[pl.ds(at * 8, 8)].reshape(256, WIDTH) for at in (core, 1 - core)
     ]
     both_rows = jnp.concatenate(rows, axis=1)
-    for k in range(2):
-        for at, size in ((0, 512), (512, 640)):
-            weight = jnp.concatenate(
-                [ref[k * WIDTH : (k + 1) * WIDTH, at : at + size] for ref in weights], axis=0
-            )
-            out_ref[:, k * UNITS + at : k * UNITS + at + size] = dot(both_rows, weight).astype(
-                bf16
-            )
+    total[...] = dot(rows[0], own_ref[:WIDTH])
+    loads[0].wait()
+    loads[1].wait()
+    for at, size in ((0, 512), (512, 640)):
+        out_ref[:, at : at + size] = (
+            total[:, at : at + size] + dot(rows[1], other_ref[:WIDTH, at : at + size])
+        ).astype(bf16)
+    loads[2].wait()
+    for at, size in ((0, 512), (512, 640)):
+        weight = jnp.concatenate(
+            [ref[WIDTH : 2 * WIDTH, at : at + size] for ref in weights], axis=0
+        )
+        out_ref[:, UNITS + at : UNITS + at + size] = dot(both_rows, weight).astype(bf16)
     squares = jnp.zeros((256, 1), f32)
     for half in range(2):
         gain = weights[half][PACK_SCALES:, :WIDTH].astype(f32)
@@ -296,11 +314,16 @@
     return pl.pallas_call(
         gate_up_kernel,
         out_shape=jax.ShapeDtypeStruct((256, 2 * UNITS + EXTRA), bf16),
-        in_specs=[VMEM] * 3,
+        in_specs=[VMEM, VMEM, HBM],
         out_specs=VMEM,
+        scratch_shapes=[
+            pltpu.VMEM((PACK_ROWS, UNITS), bf16),
+            pltpu.VMEM((256, UNITS), f32),
+            pltpu.SemaphoreType.DMA((3,)),
+        ],
         compiler_params=PARAMS,
         name="gate_up",
-    )(rows, own, other)
+    )(rows, own, in_hbm(other))
 
 
 def hidden_kernel(shares_ref, scales_ref, out_ref):
@@ -394,22 +417,24 @@
     other_o = other_core(own_o)
     own_gate_up = swap(packed)
     heads = exchange(heads, NEAR)
-    attn = exchange(repeat(heads), COLS)
+    repeated = repeat(heads)
+    (down_weight,) = stage(repeated, down_weight)
+    attn = exchange(repeated, COLS)
     attn, down_weight = lax.optimization_barrier((attn, down_weight))
     own_down = swap(down_weight)
     parts = project(attn, own_o, other_o)
     other_gate_up = other_core(own_gate_up)
     parts = exchange(parts.reshape(16, 32, WIDTH), SIDE)
     stream, rows = stream_and_spread(parts, x_in, o_scale, ffn_gain)
-    (other_gate_up,) = stage(stream, other_gate_up)
     rows = exchange(rows, SIDE)
     rows, own_down = lax.optimization_barrier((rows, own_down))
     other_down = other_core(own_down)
     shares = exchange(
         gate_up(rows, own_gate_up, other_gate_up).reshape(16, 16, 2 * UNITS + EXTRA), "b"
     )
+    shares, other_down = lax.optimization_barrier((shares, other_down))
     hidden = hidden_and_spread(shares, own_gate_up[PACK_SCALES:])
-    own_down, other_down = stage(hidden, own_down, other_down)
+    (own_down,) = stage(hidden, own_down)
     hidden = exchange(hidden, "b")
     parts = exchange(down(hidden, own_down, other_down).reshape(16, 32, WIDTH), SIDE)
     lowered = jnp.sum(parts.astype(f32), axis=0)

time: 182 us -> 181 us (level)
  waiting for transfers between devices: 80.9 us -> 71.6 us
  starting transfers between devices: 59.9 us -> 64.4 us
  blocking collectives: 22.8 us -> 25.1 us
    all_to_all x5, waiting for transfers between devices: 72.8 us -> 58.9 us  [exchange(): return lax.all_to_all(parts, axis, split_axis=0, concat_axis=0, tiled=False)]
    ppermute x3, waiting for transfers between devices: 5.87 us -> 10.4 us  [swap(): return lax.ppermute(block, ('core', 'zl'), [(0, 0), (1, 2), (2, 1), (3, 3)])]
    all_to_all x5, starting transfers between devices: 37.9 us -> 40.7 us  [exchange(): return lax.all_to_all(parts, axis, split_axis=0, concat_axis=0, tiled=False)]
    all_to_all x2, blocking collectives: 22.8 us -> 25.1 us  [exchange(): return lax.all_to_all(parts, axis, split_axis=0, concat_axis=0, tiled=False)]
  transfers between devices with their start and end apart: 11 -> 11, of which waited for: 8 -> 8; matrix products, arithmetic and copies ran while one was open for 0% -> 0% of each run, Pallas kernels for 5% -> 6%
where the time goes in v4:
time: 181 us; the launch traced here: 180 us
  waiting for transfers between devices  71.6 us (40%)
  starting transfers between devices  64.4 us (36%)
  blocking collectives  25.1 us (14%)
  Pallas kernels  15.9 us (9%)
    all_to_all x5, waiting for transfers between devices, exchange(): return lax.all_to_all(parts, axis, split_axis=0, concat_axis=0, tiled=False)  58.9 us
    all_to_all x5, starting transfers between devices, exchange(): return lax.all_to_all(parts, axis, split_axis=0, concat_axis=0, tiled=False)  40.7 us
    all_to_all x2, blocking collectives, exchange(): return lax.all_to_all(parts, axis, split_axis=0, concat_axis=0, tiled=False)  25.1 us
    ppermute x3, starting transfers between devices, swap(): return lax.ppermute(block, ('core', 'zl'), [(0, 0), (1, 2), (2, 1), (3, 3)])  14.6 us
    ppermute x3, waiting for transfers between devices, swap(): return lax.ppermute(block, ('core', 'zl'), [(0, 0), (1, 2), (2, 1), (3, 3)])  10.4 us
    ppermute x3, starting transfers between devices, other_core(): return lax.ppermute(block, 'core', [(0, 1), (1, 0)])  9.09 us
  transfers between devices with their start and end apart: 11, of which 8 were waited for; matrix products, arithmetic and copies ran while one was open for 0% of the time, Pallas kernels for 6%

profile of v4, /device:TPU:1, one launch (start us, length us, event | category | flops | bytes accessed | tf_op | source)
XLA Modules:
  0.0 179.6 jit_solution(1179493768723821988)
XLA Ops:
  0.0 5.4 %collective-permute-start = (bf16[768,384]{1,0:T(8,128)(2,1)}, bf16[768,384]{1,0:T(8,128)(2,1)}, u32[]{:S(2)}, u32[]{:S(2)}) collective-permute-start(bf16[768,384]{1,0:T(8,128)(2,1)} %param.17), channel_id=1, source_target_pairs={{0,0},{1,32},{32,1},{33,33},{2,2},{3,34},{34,3},{35,35},{4,4},{5,3... | collective-permute-start | bytes 1769480 | tf_op jit(solution)/shard_map/ppermute | solution.py:381
  6.0 3.2 %attend.1 = (bf16[8,12,128]{2,1,0:T(8,128)(2,1)S(1)}, bf16[784,1152]{1,0:T(8,128)(2,1)}) custom-call(s32[1]{0:T(128)S(6)} %copy.13.length_ref, bf16[1,12288]{1,0:T(2,128)(2,1)} %query_in.1, bf16[1,2,1024]{2,1,0:T(2,128)(2,1)} %latest_in.1, bf16[1,2,256,1024]{3,2,1,0:T(8,128)(2,1)} %cache_ref.1, bf16[768,1152]{1,0:T(8,128)(2,1)} %bitcast.5, ...), custom_call_target="tpu_custom_call" | custom-call | tf_op jit(solution)/shard_map/attend/pallas_call | solution.py:146
  9.2 4.0 %collective-permute-done.own_ref = bf16[768,384]{1,0:T(8,128)(2,1)} collective-permute-done((bf16[768,384]{1,0:T(8,128)(2,1)}, bf16[768,384]{1,0:T(8,128)(2,1)}, u32[]{:S(2)}, u32[]{:S(2)}) %collective-permute-start) | collective-permute-done | bytes 589856 | tf_op jit(solution)/shard_map/ppermute | solution.py:381
  13.3 3.6 %collective-permute-start.3 = (bf16[784,1152]{1,0:T(8,128)(2,1)}, bf16[784,1152]{1,0:T(8,128)(2,1)S(1)}, u32[]{:S(2)}, u32[]{:S(2)}) collective-permute-start(bf16[784,1152]{1,0:T(8,128)(2,1)} %get-tuple-element.27), channel_id=1, source_target_pairs={{0,0},{1,32},{32,1},{33,33},{2,2},{3,34},{34,3},{35,35},{4,4},{5,3... | collective-permute-start | bytes 5419016 | tf_op jit(solution)/shard_map/ppermute | solution.py:381
  16.9 10.2 %all_to_all.35.heads_ref = bf16[8,12,128]{2,1,0:T(8,128)(2,1)S(1)} all-to-all(bf16[8,12,128]{2,1,0:T(8,128)(2,1)S(1)} %get-tuple-element.20), channel_id=1, replica_groups=mesh['ylo'=2,'x'=4,'core'=2,'b'=16,'zl'=2] {'ylo','x'}, dimensions={0} | all-to-all | bytes 49152 | tf_op jit(solution)/shard_map/all_to_all | solution.py:389
  27.1 0.8 repeat.1.after_ref
  27.9 13.6 %all-to-all-start.1 = ((bf16[32,8,768]{2,1,0:T(8,128)(2,1)}), bf16[32,8,768]{2,1,0:T(8,128)(2,1)S(1)}, u32[]{:S(2)}, u32[]{:S(2)}) async-start(bf16[32,8,768]{2,1,0:T(8,128)(2,1)} %repeat.1.after_ref), calls=%async_computation.1 | async-start | bytes 786432 | tf_op jit(solution)/shard_map/all_to_all | solution.py:389
  41.5 2.6 %collective-permute-start.1 = (bf16[768,384]{1,0:T(8,128)(2,1)}, bf16[768,384]{1,0:T(8,128)(2,1)}, u32[]{:S(2)}, u32[]{:S(2)}) collective-permute-start(bf16[768,384]{1,0:T(8,128)(2,1)} %collective-permute-done.own_ref), channel_id=1, source_target_pairs={{0,32},{32,0},{1,33},{33,1},{2,34},{34,2},{3,35},{35,3},{4,36},{36... | collective-permute-start | bytes 1769480 | tf_op jit(solution)/shard_map/ppermute | solution.py:385
  44.1 1.9 %collective-permute-start.4 = (bf16[784,1152]{1,0:T(8,128)(2,1)S(1)}, bf16[784,1152]{1,0:T(8,128)(2,1)}, u32[]{:S(2)}, u32[]{:S(2)}) collective-permute-start(bf16[784,1152]{1,0:T(8,128)(2,1)S(1)} %collective-permute-done.3.own_ref), channel_id=1, source_target_pairs={{0,32},{32,0},{1,33},{33,1},{2,34},{34,2},{3,35},{35,3},{4,36},{36... | collective-permute-start | bytes 5419016 | tf_op jit(solution)/shard_map/ppermute | solution.py:385
  46.0 1.2 stage.2
  47.3 9.1 %all-to-all-done.1.attn_ref = bf16[32,8,768]{2,1,0:T(8,128)(2,1)S(1)} async-done(((bf16[32,8,768]{2,1,0:T(8,128)(2,1)}), bf16[32,8,768]{2,1,0:T(8,128)(2,1)S(1)}, u32[]{:S(2)}, u32[]{:S(2)}) %all-to-all-start.1) | async-done | bytes 393248 | tf_op jit(solution)/shard_map/all_to_all | solution.py:389
  56.4 3.3 %project.1 = bf16[2,256,384]{2,1,0:T(8,128)(2,1)} custom-call(bf16[32,8,768]{2,1,0:T(8,128)(2,1)S(1)} %all-to-all-done.1.attn_ref, bf16[768,384]{1,0:T(8,128)(2,1)} %collective-permute-done.own_ref, bf16[768,384]{1,0:T(8,128)(2,1)} %collective-permute-done.1.other_in), custom_call_target="tpu_custom_call" | custom-call | tf_op jit(solution)/shard_map/project/pallas_call | solution.py:211
  59.7 4.2 %all-to-all-start.2 = ((bf16[16,32,384]{2,1,0:T(8,128)(2,1)}), bf16[16,32,384]{2,1,0:T(8,128)(2,1)S(1)}, u32[]{:S(2)}, u32[]{:S(2)}) async-start(bf16[16,32,384]{2,1,0:T(8,128)(2,1)} %bitcast.1), calls=%async_computation.2 | async-start | bytes 786432 | tf_op jit(solution)/shard_map/all_to_all | solution.py:389
  63.9 5.5 %collective-permute-start.2 = (bf16[1152,384]{1,0:T(8,128)(2,1)S(1)}, bf16[1152,384]{1,0:T(8,128)(2,1)}, u32[]{:S(2)}, u32[]{:S(2)}) collective-permute-start(bf16[1152,384]{1,0:T(8,128)(2,1)S(1)} %stage.2), channel_id=1, source_target_pairs={{0,0},{1,32},{32,1},{33,33},{2,2},{3,34},{34,3},{35,35},{4,4},{5,3... | collective-permute-start | bytes 2654216 | tf_op jit(solution)/shard_map/ppermute | solution.py:381
  69.5 2.8 %all-to-all-done.2.parts_ref = bf16[16,32,384]{2,1,0:T(8,128)(2,1)S(1)} async-done(((bf16[16,32,384]{2,1,0:T(8,128)(2,1)}), bf16[16,32,384]{2,1,0:T(8,128)(2,1)S(1)}, u32[]{:S(2)}, u32[]{:S(2)}) %all-to-all-start.2) | async-done | bytes 393248 | tf_op jit(solution)/shard_map/all_to_all | solution.py:389
  72.3 0.8 stream.1
  73.1 3.6 %all-to-all-start.3 = ((bf16[16,32,384]{2,1,0:T(8,128)(2,1)}), bf16[16,32,384]{2,1,0:T(8,128)(2,1)S(1)}, u32[]{:S(2)}, u32[]{:S(2)}) async-start(bf16[16,32,384]{2,1,0:T(8,128)(2,1)} %get-tuple-element.24), calls=%async_computation.3 | async-start | bytes 786432 | tf_op jit(solution)/shard_map/all_to_all | solution.py:389
  76.7 6.4 %collective-permute-done.2.refs_0_ = bf16[1152,384]{1,0:T(8,128)(2,1)} collective-permute-done((bf16[1152,384]{1,0:T(8,128)(2,1)S(1)}, bf16[1152,384]{1,0:T(8,128)(2,1)}, u32[]{:S(2)}, u32[]{:S(2)}) %collective-permute-start.2) | collective-permute-done | bytes 884768 | tf_op jit(solution)/shard_map/ppermute | solution.py:381
  83.1 1.7 all-to-all-done.3.rows_ref
  84.7 3.6 %gate_up.1 = bf16[256,2432]{1,0:T(8,128)(2,1)} custom-call(bf16[16,32,384]{2,1,0:T(8,128)(2,1)S(1)} %all-to-all-done.3.rows_ref, bf16[784,1152]{1,0:T(8,128)(2,1)S(1)} %collective-permute-done.3.own_ref, bf16[784,1152]{1,0:T(8,128)(2,1)} %collective-permute-done.4.other_in), custom_call_target="tpu_custom_call" | custom-call | tf_op jit(solution)/shard_map/gate_up/pallas_call | solution.py:314
  88.4 9.4 %all-to-all-start.4 = ((bf16[16,16,2432]{2,1,0:T(8,128)(2,1)}), bf16[16,16,2432]{2,1,0:T(8,128)(2,1)S(1)}, u32[]{:S(2)}, u32[]{:S(2)}) async-start(bf16[16,16,2432]{2,1,0:T(8,128)(2,1)} %bitcast.2), calls=%async_computation.4 | async-start | bytes 2490368 | tf_op jit(solution)/shard_map/all_to_all | solution.py:389
  97.8 4.6 %collective-permute-start.5 = (bf16[1152,384]{1,0:T(8,128)(2,1)}, bf16[1152,384]{1,0:T(8,128)(2,1)S(1)}, u32[]{:S(2)}, u32[]{:S(2)}) collective-permute-start(bf16[1152,384]{1,0:T(8,128)(2,1)} %collective-permute-done.2.refs_0_), channel_id=1, source_target_pairs={{0,32},{32,0},{1,33},{33,1},{2,34},{34,2},{3,35},{35,3},{4,36},{36... | collective-permute-start | bytes 2654216 | tf_op jit(solution)/shard_map/ppermute | solution.py:385
  102.4 2.2 %collective-permute-done.5.other_ref = bf16[1152,384]{1,0:T(8,128)(2,1)S(1)} collective-permute-done((bf16[1152,384]{1,0:T(8,128)(2,1)}, bf16[1152,384]{1,0:T(8,128)(2,1)S(1)}, u32[]{:S(2)}, u32[]{:S(2)}) %collective-permute-start.5) | collective-permute-done | bytes 884768 | tf_op jit(solution)/shard_map/ppermute | solution.py:385
  104.7 0.9 copy-done
  105.6 25.0 %all-to-all-done.4.shares_ref = bf16[16,16,2432]{2,1,0:T(8,128)(2,1)S(1)} async-done(((bf16[16,16,2432]{2,1,0:T(8,128)(2,1)}), bf16[16,16,2432]{2,1,0:T(8,128)(2,1)S(1)}, u32[]{:S(2)}, u32[]{:S(2)}) %all-to-all-start.4) | async-done | bytes 1245216 | tf_op jit(solution)/shard_map/all_to_all | solution.py:389
  130.6 1.1 hidden.1.after_ref
  131.7 9.9 %all-to-all-start.5 = ((bf16[16,16,1152]{2,1,0:T(8,128)(2,1)}), bf16[16,16,1152]{2,1,0:T(8,128)(2,1)S(1)}, u32[]{:S(2)}, u32[]{:S(2)}) async-start(bf16[16,16,1152]{2,1,0:T(8,128)(2,1)} %hidden.1.after_ref), calls=%async_computation.5 | async-start | bytes 1179648 | tf_op jit(solution)/shard_map/all_to_all | solution.py:389
  141.6 1.2 stage.3.own_ref
  142.8 20.3 %all-to-all-done.5.hidden_ref = bf16[16,16,1152]{2,1,0:T(8,128)(2,1)S(1)} async-done(((bf16[16,16,1152]{2,1,0:T(8,128)(2,1)}), bf16[16,16,1152]{2,1,0:T(8,128)(2,1)S(1)}, u32[]{:S(2)}, u32[]{:S(2)}) %all-to-all-start.5) | async-done | bytes 589856 | tf_op jit(solution)/shard_map/all_to_all | solution.py:389
  163.1 0.8 down.1
  163.9 14.9 %all_to_all.36 = bf16[16,32,384]{2,1,0:T(8,128)(2,1)S(1)} all-to-all(bf16[16,32,384]{2,1,0:T(8,128)(2,1)S(1)} %bitcast.4), channel_id=1, replica_groups=mesh['ylo'=2,'x'=4,'core'=2,'b'=16,'zl'=2] {'zl','ylo','x'}, dimensions={0} | all-to-all | bytes 786432 | tf_op jit(solution)/shard_map/all_to_all | solution.py:389
  178.9 0.6 add_convert_fusion
  (18 shorter events, 0.1 us)
Async XLA Ops:
  0.0 13.3 %collective-permute-start = (bf16[768,384]{1,0:T(8,128)(2,1)}, bf16[768,384]{1,0:T(8,128)(2,1)}, u32[]{:S(2)}, u32[]{:S(2)}) collective-permute-start(bf16[768,384]{1,0:T(8,128)(2,1)} %param.17), channel_id=1, source_target_pairs={{0,0},{1,32},{32,1},{33,33},{2,2},{3,34},{34,3},{35,35},{4,4},{5,3... | collective-permute-start | bytes 1769480 | tf_op jit(solution)/shard_map/ppermute | solution.py:381
  13.3 30.8 %collective-permute-start.3 = (bf16[784,1152]{1,0:T(8,128)(2,1)}, bf16[784,1152]{1,0:T(8,128)(2,1)S(1)}, u32[]{:S(2)}, u32[]{:S(2)}) collective-permute-start(bf16[784,1152]{1,0:T(8,128)(2,1)} %get-tuple-element.27), channel_id=1, source_target_pairs={{0,0},{1,32},{32,1},{33,33},{2,2},{3,34},{34,3},{35,35},{4,4},{5,3... | collective-permute-start | bytes 5419016 | tf_op jit(solution)/shard_map/ppermute | solution.py:381
  27.9 28.5 %all-to-all-start.1 = ((bf16[32,8,768]{2,1,0:T(8,128)(2,1)}), bf16[32,8,768]{2,1,0:T(8,128)(2,1)S(1)}, u32[]{:S(2)}, u32[]{:S(2)}) async-start(bf16[32,8,768]{2,1,0:T(8,128)(2,1)} %repeat.1.after_ref), calls=%async_computation.1 | async-start | bytes 786432 | tf_op jit(solution)/shard_map/all_to_all | solution.py:389
  41.5 14.9 %collective-permute-start.1 = (bf16[768,384]{1,0:T(8,128)(2,1)}, bf16[768,384]{1,0:T(8,128)(2,1)}, u32[]{:S(2)}, u32[]{:S(2)}) collective-permute-start(bf16[768,384]{1,0:T(8,128)(2,1)} %collective-permute-done.own_ref), channel_id=1, source_target_pairs={{0,32},{32,0},{1,33},{33,1},{2,34},{34,2},{3,35},{35,3},{4,36},{36... | collective-permute-start | bytes 1769480 | tf_op jit(solution)/shard_map/ppermute | solution.py:385
  44.1 40.6 %collective-permute-start.4 = (bf16[784,1152]{1,0:T(8,128)(2,1)S(1)}, bf16[784,1152]{1,0:T(8,128)(2,1)}, u32[]{:S(2)}, u32[]{:S(2)}) collective-permute-start(bf16[784,1152]{1,0:T(8,128)(2,1)S(1)} %collective-permute-done.3.own_ref), channel_id=1, source_target_pairs={{0,32},{32,0},{1,33},{33,1},{2,34},{34,2},{3,35},{35,3},{4,36},{36... | collective-permute-start | bytes 5419016 | tf_op jit(solution)/shard_map/ppermute | solution.py:385
  47.2 22.2 %copy-start.3 = (f32[384]{0:T(512)S(1)}, f32[384]{0:T(512)}, u32[]{:S(2)}) copy-start(f32[384]{0:T(512)} %gain_ref.1) | copy-start | bytes 4612
  47.2 22.2 %copy-start.5 = (f32[384]{0:T(512)S(1)}, f32[384]{0:T(512)}, u32[]{:S(2)}) copy-start(f32[384]{0:T(512)} %param.18) | copy-start | bytes 4612
  47.2 25.0 %copy-start.2 = (bf16[32,384]{1,0:T(8,128)(2,1)S(1)}, bf16[32,384]{1,0:T(8,128)(2,1)}, u32[]{:S(2)}) copy-start(bf16[32,384]{1,0:T(8,128)(2,1)} %x_ref.1) | copy-start | bytes 73732
  59.7 12.6 %all-to-all-start.2 = ((bf16[16,32,384]{2,1,0:T(8,128)(2,1)}), bf16[16,32,384]{2,1,0:T(8,128)(2,1)S(1)}, u32[]{:S(2)}, u32[]{:S(2)}) async-start(bf16[16,32,384]{2,1,0:T(8,128)(2,1)} %bitcast.1), calls=%async_computation.2 | async-start | bytes 786432 | tf_op jit(solution)/shard_map/all_to_all | solution.py:389
  63.9 19.2 %collective-permute-start.2 = (bf16[1152,384]{1,0:T(8,128)(2,1)S(1)}, bf16[1152,384]{1,0:T(8,128)(2,1)}, u32[]{:S(2)}, u32[]{:S(2)}) collective-permute-start(bf16[1152,384]{1,0:T(8,128)(2,1)S(1)} %stage.2), channel_id=1, source_target_pairs={{0,0},{1,32},{32,1},{33,33},{2,2},{3,34},{34,3},{35,35},{4,4},{5,3... | collective-permute-start | bytes 2654216 | tf_op jit(solution)/shard_map/ppermute | solution.py:381
  73.1 11.6 %all-to-all-start.3 = ((bf16[16,32,384]{2,1,0:T(8,128)(2,1)}), bf16[16,32,384]{2,1,0:T(8,128)(2,1)S(1)}, u32[]{:S(2)}, u32[]{:S(2)}) async-start(bf16[16,32,384]{2,1,0:T(8,128)(2,1)} %get-tuple-element.24), calls=%async_computation.3 | async-start | bytes 786432 | tf_op jit(solution)/shard_map/all_to_all | solution.py:389
  88.4 42.2 %all-to-all-start.4 = ((bf16[16,16,2432]{2,1,0:T(8,128)(2,1)}), bf16[16,16,2432]{2,1,0:T(8,128)(2,1)S(1)}, u32[]{:S(2)}, u32[]{:S(2)}) async-start(bf16[16,16,2432]{2,1,0:T(8,128)(2,1)} %bitcast.2), calls=%async_computation.4 | async-start | bytes 2490368 | tf_op jit(solution)/shard_map/all_to_all | solution.py:389
  97.8 6.9 %collective-permute-start.5 = (bf16[1152,384]{1,0:T(8,128)(2,1)}, bf16[1152,384]{1,0:T(8,128)(2,1)S(1)}, u32[]{:S(2)}, u32[]{:S(2)}) collective-permute-start(bf16[1152,384]{1,0:T(8,128)(2,1)} %collective-permute-done.2.refs_0_), channel_id=1, source_target_pairs={{0,32},{32,0},{1,33},{33,1},{2,34},{34,2},{3,35},{35,3},{4,36},{36... | collective-permute-start | bytes 2654216 | tf_op jit(solution)/shard_map/ppermute | solution.py:385
  104.7 0.9 copy-start
  131.7 31.4 %copy-start.1 = (bf16[1152,384]{1,0:T(8,128)(2,1)S(1)}, bf16[1152,384]{1,0:T(8,128)(2,1)}, u32[]{:S(2)}) copy-start(bf16[1152,384]{1,0:T(8,128)(2,1)} %copy-done) | copy-start | bytes 2654212
  131.7 31.4 %all-to-all-start.5 = ((bf16[16,16,1152]{2,1,0:T(8,128)(2,1)}), bf16[16,16,1152]{2,1,0:T(8,128)(2,1)S(1)}, u32[]{:S(2)}, u32[]{:S(2)}) async-start(bf16[16,16,1152]{2,1,0:T(8,128)(2,1)} %hidden.1.after_ref), calls=%async_computation.5 | async-start | bytes 1179648 | tf_op jit(solution)/shard_map/all_to_all | solution.py:389
  142.8 36.1 %copy-start.4 = (f32[384]{0:T(512)S(1)}, f32[384]{0:T(512)}, u32[]{:S(2)}) copy-start(f32[384]{0:T(512)} %param.23) | copy-start | bytes 4612

commit v5 on v4

--- a/solution.py
+++ b/solution.py
@@ -193,17 +193,22 @@
     )(heads)
 
 
-def project_kernel(attn_ref, own_ref, other_in, out_ref, other_ref, sem):
-    load = pltpu.make_async_copy(other_in, other_ref, sem.at[0])
-    load.start()
+def project_kernel(attn_ref, own_in, other_in, out_ref, own_ref, other_ref, sems):
+    loads = [
+        pltpu.make_async_copy(own_in, own_ref, sems.at[0]),
+        pltpu.make_async_copy(other_in, other_ref, sems.at[1]),
+    ]
+    for load in loads:
+        load.start()
     row = lax.broadcasted_iota(jnp.int32, (256, 256), 0)
     source = (row & 31) * 8 + (row >> 5)
     pick = (lax.broadcasted_iota(jnp.int32, (256, 256), 1) == source).astype(f32).astype(bf16)
     attn = attn_ref[...].astype(f32).reshape(256, 768).astype(bf16)
     attn = dot(pick, attn).astype(bf16)
     core = lax.axis_index("core")
+    loads[0].wait()
     out_ref[core] = dot(attn, own_ref[...]).astype(bf16)
-    load.wait()
+    loads[1].wait()
     out_ref[1 - core] = dot(attn, other_ref[...]).astype(bf16)
 
 
@@ -211,12 +216,16 @@
     return pl.pallas_call(
         project_kernel,
         out_shape=jax.ShapeDtypeStruct((2, 256, WIDTH), bf16),
-        in_specs=[VMEM, VMEM, HBM],
+        in_specs=[VMEM, HBM, HBM],
         out_specs=VMEM,
-        scratch_shapes=[pltpu.VMEM((768, WIDTH), bf16), pltpu.SemaphoreType.DMA((1,))],
+        scratch_shapes=[
+            pltpu.VMEM((768, WIDTH), bf16),
+            pltpu.VMEM((768, WIDTH), bf16),
+            pltpu.SemaphoreType.DMA((2,)),
+        ],
         compiler_params=PARAMS,
         name="project",
-    )(attn, own, in_hbm(other))
+    )(attn, in_hbm(own), in_hbm(other))
 
 
 def stream_kernel(parts_ref, x_ref, scale_ref, gain_ref, stream_ref, out_ref):
@@ -403,6 +412,7 @@
     down_weight,
     down_scale,
 ):
+    (o_weight,) = stage(in_hbm(key_value_cache), o_weight)
     own_o = swap(o_weight)
     heads, packed = attend(
         query,

time: 181 us -> 180 us (level)
  waiting for transfers between devices: 71.6 us -> 68.5 us
    all_to_all x5, waiting for transfers between devices: 58.9 us -> 56.1 us  [exchange(): return lax.all_to_all(parts, axis, split_axis=0, concat_axis=0, tiled=False)]
  transfers between devices with their start and end apart: 11 -> 11, of which waited for: 8 -> 8; matrix products, arithmetic and copies ran while one was open for 0% -> 0% of each run, Pallas kernels for 6% -> 5%
where the time goes in v5:
time: 180 us; the launch traced here: 179 us
  waiting for transfers between devices  68.5 us (38%)
  starting transfers between devices  64.6 us (36%)
  blocking collectives  26.8 us (15%)
  Pallas kernels  16.4 us (9%)
    all_to_all x5, waiting for transfers between devices, exchange(): return lax.all_to_all(parts, axis, split_axis=0, concat_axis=0, tiled=False)  56.1 us
    all_to_all x5, starting transfers between devices, exchange(): return lax.all_to_all(parts, axis, split_axis=0, concat_axis=0, tiled=False)  40.9 us
    all_to_all x2, blocking collectives, exchange(): return lax.all_to_all(parts, axis, split_axis=0, concat_axis=0, tiled=False)  26.8 us
    ppermute x3, starting transfers between devices, swap(): return lax.ppermute(block, ('core', 'zl'), [(0, 0), (1, 2), (2, 1), (3, 3)])  14.6 us
    ppermute x3, waiting for transfers between devices, swap(): return lax.ppermute(block, ('core', 'zl'), [(0, 0), (1, 2), (2, 1), (3, 3)])  10.2 us
    ppermute x3, starting transfers between devices, other_core(): return lax.ppermute(block, 'core', [(0, 1), (1, 0)])  9.1 us
    pallas_call x1, Pallas kernels, gate_up(): pl.pallas_call(gate_up_kernel, out_shape=jax.ShapeDtypeStruct((256, 2 * U...  3.62 us
  transfers between devices with their start and end apart: 11, of which 8 were waited for; matrix products, arithmetic and copies ran while one was open for 0% of the time, Pallas kernels for 5%

profile of v5, /device:TPU:1, one launch (start us, length us, event | category | flops | bytes accessed | tf_op | source)
XLA Modules:
  0.0 178.8 jit_solution(8342629936930968361)
XLA Ops:
  0.0 1.1 stage.3
  1.1 5.4 %collective-permute-start = (bf16[768,384]{1,0:T(8,128)(2,1)S(1)}, bf16[768,384]{1,0:T(8,128)(2,1)}, u32[]{:S(2)}, u32[]{:S(2)}) collective-permute-start(bf16[768,384]{1,0:T(8,128)(2,1)S(1)} %stage.3), channel_id=1, source_target_pairs={{0,0},{1,32},{32,1},{33,33},{2,2},{3,34},{34,3},{35,35},{4,4},{5,3... | collective-permute-start | bytes 1769480 | tf_op jit(solution)/shard_map/ppermute | solution.py:390
  7.1 3.2 %attend.1 = (bf16[8,12,128]{2,1,0:T(8,128)(2,1)S(1)}, bf16[784,1152]{1,0:T(8,128)(2,1)}) custom-call(s32[1]{0:T(128)S(6)} %copy.13.length_ref, bf16[1,12288]{1,0:T(2,128)(2,1)} %query_in.1, bf16[1,2,1024]{2,1,0:T(2,128)(2,1)} %latest_in.1, bf16[1,2,256,1024]{3,2,1,0:T(8,128)(2,1)} %after_ref.1, bf16[768,1152]{1,0:T(8,128)(2,1)} %bitcast.5, ...), custom_call_target="tpu_custom_call" | custom-call | tf_op jit(solution)/shard_map/attend/pallas_call | solution.py:146
  10.3 3.8 %collective-permute-done.own_in = bf16[768,384]{1,0:T(8,128)(2,1)} collective-permute-done((bf16[768,384]{1,0:T(8,128)(2,1)S(1)}, bf16[768,384]{1,0:T(8,128)(2,1)}, u32[]{:S(2)}, u32[]{:S(2)}) %collective-permute-start) | collective-permute-done | bytes 589856 | tf_op jit(solution)/shard_map/ppermute | solution.py:390
  14.1 3.6 %collective-permute-start.3 = (bf16[784,1152]{1,0:T(8,128)(2,1)}, bf16[784,1152]{1,0:T(8,128)(2,1)S(1)}, u32[]{:S(2)}, u32[]{:S(2)}) collective-permute-start(bf16[784,1152]{1,0:T(8,128)(2,1)} %get-tuple-element.27), channel_id=1, source_target_pairs={{0,0},{1,32},{32,1},{33,33},{2,2},{3,34},{34,3},{35,35},{4,4},{5,3... | collective-permute-start | bytes 5419016 | tf_op jit(solution)/shard_map/ppermute | solution.py:390
  17.8 9.9 %all_to_all.35.heads_ref = bf16[8,12,128]{2,1,0:T(8,128)(2,1)S(1)} all-to-all(bf16[8,12,128]{2,1,0:T(8,128)(2,1)S(1)} %get-tuple-element.20), channel_id=1, replica_groups=mesh['ylo'=2,'x'=4,'core'=2,'b'=16,'zl'=2] {'ylo','x'}, dimensions={0} | all-to-all | bytes 49152 | tf_op jit(solution)/shard_map/all_to_all | solution.py:398
  27.7 0.8 repeat.1.after_ref
  28.5 13.9 %all-to-all-start.1 = ((bf16[32,8,768]{2,1,0:T(8,128)(2,1)}), bf16[32,8,768]{2,1,0:T(8,128)(2,1)S(1)}, u32[]{:S(2)}, u32[]{:S(2)}) async-start(bf16[32,8,768]{2,1,0:T(8,128)(2,1)} %repeat.1.after_ref), calls=%async_computation.1 | async-start | bytes 786432 | tf_op jit(solution)/shard_map/all_to_all | solution.py:398
  42.4 2.6 %collective-permute-start.1 = (bf16[768,384]{1,0:T(8,128)(2,1)}, bf16[768,384]{1,0:T(8,128)(2,1)}, u32[]{:S(2)}, u32[]{:S(2)}) collective-permute-start(bf16[768,384]{1,0:T(8,128)(2,1)} %collective-permute-done.own_in), channel_id=1, source_target_pairs={{0,32},{32,0},{1,33},{33,1},{2,34},{34,2},{3,35},{35,3},{4,36},{36... | collective-permute-start | bytes 1769480 | tf_op jit(solution)/shard_map/ppermute | solution.py:394
  45.0 1.9 %collective-permute-start.4 = (bf16[784,1152]{1,0:T(8,128)(2,1)S(1)}, bf16[784,1152]{1,0:T(8,128)(2,1)}, u32[]{:S(2)}, u32[]{:S(2)}) collective-permute-start(bf16[784,1152]{1,0:T(8,128)(2,1)S(1)} %collective-permute-done.3.own_ref), channel_id=1, source_target_pairs={{0,32},{32,0},{1,33},{33,1},{2,34},{34,2},{3,35},{35,3},{4,36},{36... | collective-permute-start | bytes 5419016 | tf_op jit(solution)/shard_map/ppermute | solution.py:394
  46.9 1.2 stage.4
  48.1 9.1 %all-to-all-done.1.attn_ref = bf16[32,8,768]{2,1,0:T(8,128)(2,1)S(1)} async-done(((bf16[32,8,768]{2,1,0:T(8,128)(2,1)}), bf16[32,8,768]{2,1,0:T(8,128)(2,1)S(1)}, u32[]{:S(2)}, u32[]{:S(2)}) %all-to-all-start.1) | async-done | bytes 393248 | tf_op jit(solution)/shard_map/all_to_all | solution.py:398
  57.3 2.6 %project.1 = bf16[2,256,384]{2,1,0:T(8,128)(2,1)} custom-call(bf16[32,8,768]{2,1,0:T(8,128)(2,1)S(1)} %all-to-all-done.1.attn_ref, bf16[768,384]{1,0:T(8,128)(2,1)} %collective-permute-done.own_in, bf16[768,384]{1,0:T(8,128)(2,1)} %collective-permute-done.1.other_in), custom_call_target="tpu_custom_call" | custom-call | tf_op jit(solution)/shard_map/project/pallas_call | solution.py:216
  59.9 4.2 %all-to-all-start.2 = ((bf16[16,32,384]{2,1,0:T(8,128)(2,1)}), bf16[16,32,384]{2,1,0:T(8,128)(2,1)S(1)}, u32[]{:S(2)}, u32[]{:S(2)}) async-start(bf16[16,32,384]{2,1,0:T(8,128)(2,1)} %bitcast.1), calls=%async_computation.2 | async-start | bytes 786432 | tf_op jit(solution)/shard_map/all_to_all | solution.py:398
  64.1 5.5 %collective-permute-start.2 = (bf16[1152,384]{1,0:T(8,128)(2,1)S(1)}, bf16[1152,384]{1,0:T(8,128)(2,1)}, u32[]{:S(2)}, u32[]{:S(2)}) collective-permute-start(bf16[1152,384]{1,0:T(8,128)(2,1)S(1)} %stage.4), channel_id=1, source_target_pairs={{0,0},{1,32},{32,1},{33,33},{2,2},{3,34},{34,3},{35,35},{4,4},{5,3... | collective-permute-start | bytes 2654216 | tf_op jit(solution)/shard_map/ppermute | solution.py:390
  69.7 2.8 %all-to-all-done.2.parts_ref = bf16[16,32,384]{2,1,0:T(8,128)(2,1)S(1)} async-done(((bf16[16,32,384]{2,1,0:T(8,128)(2,1)}), bf16[16,32,384]{2,1,0:T(8,128)(2,1)S(1)}, u32[]{:S(2)}, u32[]{:S(2)}) %all-to-all-start.2) | async-done | bytes 393248 | tf_op jit(solution)/shard_map/all_to_all | solution.py:398
  72.5 0.8 stream.1
  73.4 3.6 %all-to-all-start.3 = ((bf16[16,32,384]{2,1,0:T(8,128)(2,1)}), bf16[16,32,384]{2,1,0:T(8,128)(2,1)S(1)}, u32[]{:S(2)}, u32[]{:S(2)}) async-start(bf16[16,32,384]{2,1,0:T(8,128)(2,1)} %get-tuple-element.24), calls=%async_computation.3 | async-start | bytes 786432 | tf_op jit(solution)/shard_map/all_to_all | solution.py:398
  76.9 6.4 %collective-permute-done.2.refs_0_ = bf16[1152,384]{1,0:T(8,128)(2,1)} collective-permute-done((bf16[1152,384]{1,0:T(8,128)(2,1)S(1)}, bf16[1152,384]{1,0:T(8,128)(2,1)}, u32[]{:S(2)}, u32[]{:S(2)}) %collective-permute-start.2) | collective-permute-done | bytes 884768 | tf_op jit(solution)/shard_map/ppermute | solution.py:390
  83.3 1.7 all-to-all-done.3.rows_ref
  85.0 3.6 %gate_up.1 = bf16[256,2432]{1,0:T(8,128)(2,1)} custom-call(bf16[16,32,384]{2,1,0:T(8,128)(2,1)S(1)} %all-to-all-done.3.rows_ref, bf16[784,1152]{1,0:T(8,128)(2,1)S(1)} %collective-permute-done.3.own_ref, bf16[784,1152]{1,0:T(8,128)(2,1)} %collective-permute-done.4.other_in), custom_call_target="tpu_custom_call" | custom-call | tf_op jit(solution)/shard_map/gate_up/pallas_call | solution.py:323
  88.6 9.4 %all-to-all-start.4 = ((bf16[16,16,2432]{2,1,0:T(8,128)(2,1)}), bf16[16,16,2432]{2,1,0:T(8,128)(2,1)S(1)}, u32[]{:S(2)}, u32[]{:S(2)}) async-start(bf16[16,16,2432]{2,1,0:T(8,128)(2,1)} %bitcast.2), calls=%async_computation.4 | async-start | bytes 2490368 | tf_op jit(solution)/shard_map/all_to_all | solution.py:398
  98.1 4.6 %collective-permute-start.5 = (bf16[1152,384]{1,0:T(8,128)(2,1)}, bf16[1152,384]{1,0:T(8,128)(2,1)S(1)}, u32[]{:S(2)}, u32[]{:S(2)}) collective-permute-start(bf16[1152,384]{1,0:T(8,128)(2,1)} %collective-permute-done.2.refs_0_), channel_id=1, source_target_pairs={{0,32},{32,0},{1,33},{33,1},{2,34},{34,2},{3,35},{35,3},{4,36},{36... | collective-permute-start | bytes 2654216 | tf_op jit(solution)/shard_map/ppermute | solution.py:394
  102.7 2.2 %collective-permute-done.5.other_ref = bf16[1152,384]{1,0:T(8,128)(2,1)S(1)} collective-permute-done((bf16[1152,384]{1,0:T(8,128)(2,1)}, bf16[1152,384]{1,0:T(8,128)(2,1)S(1)}, u32[]{:S(2)}, u32[]{:S(2)}) %collective-permute-start.5) | collective-permute-done | bytes 884768 | tf_op jit(solution)/shard_map/ppermute | solution.py:394
  104.9 0.9 copy-done
  105.8 25.1 %all-to-all-done.4.shares_ref = bf16[16,16,2432]{2,1,0:T(8,128)(2,1)S(1)} async-done(((bf16[16,16,2432]{2,1,0:T(8,128)(2,1)}), bf16[16,16,2432]{2,1,0:T(8,128)(2,1)S(1)}, u32[]{:S(2)}, u32[]{:S(2)}) %all-to-all-start.4) | async-done | bytes 1245216 | tf_op jit(solution)/shard_map/all_to_all | solution.py:398
  130.9 1.1 hidden.1.after_ref
  132.0 9.8 %all-to-all-start.5 = ((bf16[16,16,1152]{2,1,0:T(8,128)(2,1)}), bf16[16,16,1152]{2,1,0:T(8,128)(2,1)S(1)}, u32[]{:S(2)}, u32[]{:S(2)}) async-start(bf16[16,16,1152]{2,1,0:T(8,128)(2,1)} %hidden.1.after_ref), calls=%async_computation.5 | async-start | bytes 1179648 | tf_op jit(solution)/shard_map/all_to_all | solution.py:398
  141.8 1.2 stage.5.own_ref
  143.0 17.4 %all-to-all-done.5.hidden_ref = bf16[16,16,1152]{2,1,0:T(8,128)(2,1)S(1)} async-done(((bf16[16,16,1152]{2,1,0:T(8,128)(2,1)}), bf16[16,16,1152]{2,1,0:T(8,128)(2,1)S(1)}, u32[]{:S(2)}, u32[]{:S(2)}) %all-to-all-start.5) | async-done | bytes 589856 | tf_op jit(solution)/shard_map/all_to_all | solution.py:398
  160.4 0.8 down.1
  161.3 16.8 %all_to_all.36 = bf16[16,32,384]{2,1,0:T(8,128)(2,1)S(1)} all-to-all(bf16[16,32,384]{2,1,0:T(8,128)(2,1)S(1)} %bitcast.4), channel_id=1, replica_groups=mesh['ylo'=2,'x'=4,'core'=2,'b'=16,'zl'=2] {'zl','ylo','x'}, dimensions={0} | all-to-all | bytes 786432 | tf_op jit(solution)/shard_map/all_to_all | solution.py:398
  (19 shorter events, 0.7 us)
Async XLA Ops:
  1.1 13.1 %collective-permute-start = (bf16[768,384]{1,0:T(8,128)(2,1)S(1)}, bf16[768,384]{1,0:T(8,128)(2,1)}, u32[]{:S(2)}, u32[]{:S(2)}) collective-permute-start(bf16[768,384]{1,0:T(8,128)(2,1)S(1)} %stage.3), channel_id=1, source_target_pairs={{0,0},{1,32},{32,1},{33,33},{2,2},{3,34},{34,3},{35,35},{4,4},{5,3... | collective-permute-start | bytes 1769480 | tf_op jit(solution)/shard_map/ppermute | solution.py:390
  14.1 30.8 %collective-permute-start.3 = (bf16[784,1152]{1,0:T(8,128)(2,1)}, bf16[784,1152]{1,0:T(8,128)(2,1)S(1)}, u32[]{:S(2)}, u32[]{:S(2)}) collective-permute-start(bf16[784,1152]{1,0:T(8,128)(2,1)} %get-tuple-element.27), channel_id=1, source_target_pairs={{0,0},{1,32},{32,1},{33,33},{2,2},{3,34},{34,3},{35,35},{4,4},{5,3... | collective-permute-start | bytes 5419016 | tf_op jit(solution)/shard_map/ppermute | solution.py:390
  28.5 28.8 %all-to-all-start.1 = ((bf16[32,8,768]{2,1,0:T(8,128)(2,1)}), bf16[32,8,768]{2,1,0:T(8,128)(2,1)S(1)}, u32[]{:S(2)}, u32[]{:S(2)}) async-start(bf16[32,8,768]{2,1,0:T(8,128)(2,1)} %repeat.1.after_ref), calls=%async_computation.1 | async-start | bytes 786432 | tf_op jit(solution)/shard_map/all_to_all | solution.py:398
  42.4 14.9 %collective-permute-start.1 = (bf16[768,384]{1,0:T(8,128)(2,1)}, bf16[768,384]{1,0:T(8,128)(2,1)}, u32[]{:S(2)}, u32[]{:S(2)}) collective-permute-start(bf16[768,384]{1,0:T(8,128)(2,1)} %collective-permute-done.own_in), channel_id=1, source_target_pairs={{0,32},{32,0},{1,33},{33,1},{2,34},{34,2},{3,35},{35,3},{4,36},{36... | collective-permute-start | bytes 1769480 | tf_op jit(solution)/shard_map/ppermute | solution.py:394
  45.0 40.0 %collective-permute-start.4 = (bf16[784,1152]{1,0:T(8,128)(2,1)S(1)}, bf16[784,1152]{1,0:T(8,128)(2,1)}, u32[]{:S(2)}, u32[]{:S(2)}) collective-permute-start(bf16[784,1152]{1,0:T(8,128)(2,1)S(1)} %collective-permute-done.3.own_ref), channel_id=1, source_target_pairs={{0,32},{32,0},{1,33},{33,1},{2,34},{34,2},{3,35},{35,3},{4,36},{36... | collective-permute-start | bytes 5419016 | tf_op jit(solution)/shard_map/ppermute | solution.py:394
  48.1 21.6 %copy-start.3 = (f32[384]{0:T(512)S(1)}, f32[384]{0:T(512)}, u32[]{:S(2)}) copy-start(f32[384]{0:T(512)} %gain_ref.1) | copy-start | bytes 4612
  48.1 21.6 %copy-start.5 = (f32[384]{0:T(512)S(1)}, f32[384]{0:T(512)}, u32[]{:S(2)}) copy-start(f32[384]{0:T(512)} %param.18) | copy-start | bytes 4612
  48.1 24.4 %copy-start.2 = (bf16[32,384]{1,0:T(8,128)(2,1)S(1)}, bf16[32,384]{1,0:T(8,128)(2,1)}, u32[]{:S(2)}) copy-start(bf16[32,384]{1,0:T(8,128)(2,1)} %x_ref.1) | copy-start | bytes 73732
  59.9 12.6 %all-to-all-start.2 = ((bf16[16,32,384]{2,1,0:T(8,128)(2,1)}), bf16[16,32,384]{2,1,0:T(8,128)(2,1)S(1)}, u32[]{:S(2)}, u32[]{:S(2)}) async-start(bf16[16,32,384]{2,1,0:T(8,128)(2,1)} %bitcast.1), calls=%async_computation.2 | async-start | bytes 786432 | tf_op jit(solution)/shard_map/all_to_all | solution.py:398
  64.1 19.2 %collective-permute-start.2 = (bf16[1152,384]{1,0:T(8,128)(2,1)S(1)}, bf16[1152,384]{1,0:T(8,128)(2,1)}, u32[]{:S(2)}, u32[]{:S(2)}) collective-permute-start(bf16[1152,384]{1,0:T(8,128)(2,1)S(1)} %stage.4), channel_id=1, source_target_pairs={{0,0},{1,32},{32,1},{33,33},{2,2},{3,34},{34,3},{35,35},{4,4},{5,3... | collective-permute-start | bytes 2654216 | tf_op jit(solution)/shard_map/ppermute | solution.py:390
  73.4 11.6 %all-to-all-start.3 = ((bf16[16,32,384]{2,1,0:T(8,128)(2,1)}), bf16[16,32,384]{2,1,0:T(8,128)(2,1)S(1)}, u32[]{:S(2)}, u32[]{:S(2)}) async-start(bf16[16,32,384]{2,1,0:T(8,128)(2,1)} %get-tuple-element.24), calls=%async_computation.3 | async-start | bytes 786432 | tf_op jit(solution)/shard_map/all_to_all | solution.py:398
  88.6 42.3 %all-to-all-start.4 = ((bf16[16,16,2432]{2,1,0:T(8,128)(2,1)}), bf16[16,16,2432]{2,1,0:T(8,128)(2,1)S(1)}, u32[]{:S(2)}, u32[]{:S(2)}) async-start(bf16[16,16,2432]{2,1,0:T(8,128)(2,1)} %bitcast.2), calls=%async_computation.4 | async-start | bytes 2490368 | tf_op jit(solution)/shard_map/all_to_all | solution.py:398
  98.1 6.9 %collective-permute-start.5 = (bf16[1152,384]{1,0:T(8,128)(2,1)}, bf16[1152,384]{1,0:T(8,128)(2,1)S(1)}, u32[]{:S(2)}, u32[]{:S(2)}) collective-permute-start(bf16[1152,384]{1,0:T(8,128)(2,1)} %collective-permute-done.2.refs_0_), channel_id=1, source_target_pairs={{0,32},{32,0},{1,33},{33,1},{2,34},{34,2},{3,35},{35,3},{4,36},{36... | collective-permute-start | bytes 2654216 | tf_op jit(solution)/shard_map/ppermute | solution.py:394
  104.9 0.9 copy-start
  132.0 28.5 %copy-start.1 = (bf16[1152,384]{1,0:T(8,128)(2,1)S(1)}, bf16[1152,384]{1,0:T(8,128)(2,1)}, u32[]{:S(2)}) copy-start(bf16[1152,384]{1,0:T(8,128)(2,1)} %copy-done) | copy-start | bytes 2654212
  132.0 28.5 %all-to-all-start.5 = ((bf16[16,16,1152]{2,1,0:T(8,128)(2,1)}), bf16[16,16,1152]{2,1,0:T(8,128)(2,1)S(1)}, u32[]{:S(2)}, u32[]{:S(2)}) async-start(bf16[16,16,1152]{2,1,0:T(8,128)(2,1)} %hidden.1.after_ref), calls=%async_computation.5 | async-start | bytes 1179648 | tf_op jit(solution)/shard_map/all_to_all | solution.py:398
  143.0 35.1 %copy-start.4 = (f32[384]{0:T(512)S(1)}, f32[384]{0:T(512)}, u32[]{:S(2)}) copy-start(f32[384]{0:T(512)} %param.23) | copy-start | bytes 4612
